TPU v7x, 256 devices: a whole 4x4x8 slice. The times are simulated.
256 devices in a mesh: expert: 64 (over x, z, core), pipe: 4 (over y).
Axes of the slice: x: 4, y: 4, z: 8, core: 2. Of those that a mesh axis runs over, the one named last changes fastest.
Arguments:
- section_input: bfloat16 [4, 8192, 7168], P('pipe', 'expert'), may hold values from -6 to 6
- cotangent: bfloat16 [4, 8192, 7168], P('pipe', 'expert'), may hold values from -6 to 6
- routes: int32 [4, 8192, 8], P('pipe', 'expert'), may hold values from 0 to 255, as said below
- gate_codes: int32 [4, 8192, 8], P('pipe', 'expert'), may hold values from 1 to 256
- w_gate: bfloat16 [4, 7168, 8192], P('pipe', None, 'expert'), may hold values from -0.0625 to 0.0625
- w_up: bfloat16 [4, 7168, 8192], P('pipe', None, 'expert'), may hold values from -0.0625 to 0.0625
- w_down: bfloat16 [4, 8192, 7168], P('pipe', 'expert'), may hold values from -0.125 to 0.125
Outputs:
- next_section_input: bfloat16 [4, 8192, 7168], P('pipe', 'expert')
- prev_section_grad: bfloat16 [4, 8192, 7168], P('pipe', 'expert')
Inputs may be any that keep to these rules, and one draw needn't show every extreme that they name: `routes`: each token names 8 different experts. Of the 128 tokens of one block, at most 4 name any one expert below 4; in every section some expert below 4 is named by exactly 4 tokens of every block.
All inputs are finite; a program needn't handle non-finite values.
Results may differ from a plain program's by a relative error of at most 0.011.
Values may be sent and summed in bfloat16 or wider, within the bound.
A program may use at most 128 MiB of HBM per device.

v0:
```python
import jax
import jax.numpy as jnp
from jax import lax
from jax.sharding import PartitionSpec as P

FF = 2048
CAP = 4


def from_behind(block, axis, distance):
    devices = range(lax.axis_size(axis))
    route = [((i - distance) % len(devices), i) for i in devices]
    return lax.ppermute(block, axis, route)


def contract_rows(left, right):
    return lax.dot_general(
        left, right, (((1,), (1,)), ((), ())), preferred_element_type=jnp.float32
    )


def on_device(section_input, cotangent, routes, gate_codes, w_gate, w_up, w_down):
    highest = lax.Precision.HIGHEST
    tokens_in = section_input[0]
    grads_in = cotangent[0]
    route_ids = routes[0]
    codes_float = gate_codes[0].astype(jnp.float32)
    gate_cols = w_gate[0]
    up_cols = w_up[0]
    down_rows = w_down[0]
    devices = lax.axis_size("expert")
    hidden_dev = gate_cols.shape[1]
    group = FF // hidden_dev
    flight = devices // group
    width = tokens_in.shape[1]
    route_weight = 2.5 * codes_float / jnp.sum(codes_float, axis=-1, keepdims=True)
    named = route_ids[:, :, None] == jnp.arange(flight, dtype=jnp.int32)
    matched = jnp.sum(named, axis=1)
    token_weight = jnp.sum(jnp.where(named, route_weight[:, :, None], 0.0), axis=1)
    position = jnp.cumsum(matched, axis=0) - 1
    selector = (matched.T[:, None, :] == 1) & (
        position.T[:, None, :] == jnp.arange(CAP, dtype=jnp.int32)[None, :, None]
    )
    picks = selector.astype(jnp.bfloat16)
    picks_wide = selector.astype(jnp.float32)
    send_rows = jnp.einsum(
        "fct,td->fcd", picks, tokens_in, preferred_element_type=jnp.float32
    ).astype(jnp.bfloat16)
    slot_weight = jnp.einsum("fct,tf->fc", picks_wide, token_weight, precision=highest)
    grad_slots = jnp.einsum("fct,td->fcd", picks, grads_in, preferred_element_type=jnp.float32)
    send_grads = (slot_weight[:, :, None] * grad_slots).astype(jnp.bfloat16)
    spread_rows = jnp.repeat(send_rows, group, axis=0)
    spread_grads = jnp.repeat(send_grads, group, axis=0)
    arrived_rows = lax.all_to_all(spread_rows, "expert", split_axis=0, concat_axis=0, tiled=True)
    count = arrived_rows.shape[1]
    flat = arrived_rows.reshape(-1, width)
    gate = jnp.dot(flat, gate_cols, preferred_element_type=jnp.float32)
    upper = jnp.dot(flat, up_cols, preferred_element_type=jnp.float32)
    hidden = (jax.nn.silu(gate) * upper).astype(jnp.bfloat16)
    partial_value = jnp.dot(hidden, down_rows, preferred_element_type=jnp.float32).astype(
        jnp.bfloat16
    )
    return_partial_value = partial_value.reshape(devices, count, width)
    returned_part = lax.all_to_all(
        return_partial_value, "expert", split_axis=0, concat_axis=0, tiled=True
    )
    returned, gate, upper = (
        returned_part,
        gate.reshape(devices, count, hidden_dev),
        upper.reshape(devices, count, hidden_dev),
    )
    grad_rows = lax.all_to_all(spread_grads, "expert", split_axis=0, concat_axis=0, tiled=True)
    gate_flat = gate.reshape(-1, hidden_dev)
    upper_flat = upper.reshape(-1, hidden_dev)
    d_hidden = contract_rows(grad_rows.reshape(-1, width), down_rows)
    sigma = jax.nn.sigmoid(gate_flat)
    d_gate = (d_hidden * upper_flat * sigma * (1.0 + gate_flat * (1.0 - sigma))).astype(
        jnp.bfloat16
    )
    d_up = (d_hidden * jax.nn.silu(gate_flat)).astype(jnp.bfloat16)
    grad_part = (contract_rows(d_gate, gate_cols) + contract_rows(d_up, up_cols)).astype(
        jnp.bfloat16
    )
    grad_back = lax.all_to_all(
        grad_part.reshape(devices, CAP, width), "expert", split_axis=0, concat_axis=0, tiled=True
    )
    out_sum = jnp.sum(returned.astype(jnp.float32).reshape(flight, group, CAP, width), axis=1)
    layer_out = jnp.einsum(
        "fct,fcd->td", picks_wide, out_sum * slot_weight[:, :, None], precision=highest
    ).astype(jnp.bfloat16)
    grad_sum = jnp.sum(grad_back.astype(jnp.float32).reshape(flight, group, CAP, width), axis=1)
    input_grad = jnp.einsum("fct,fcd->td", picks_wide, grad_sum, precision=highest).astype(
        jnp.bfloat16
    )
    passed = from_behind(layer_out[None], "pipe", 1)
    grad_passed = from_behind(input_grad[None], "pipe", -1)
    return (passed, grad_passed)


def solution(mesh):
    placed = (
        P("pipe", "expert", None),
        P("pipe", "expert", None),
        P("pipe", "expert", None),
        P("pipe", "expert", None),
        P("pipe", None, "expert"),
        P("pipe", None, "expert"),
        P("pipe", "expert", None),
    )
    return jax.shard_map(
        on_device,
        mesh=mesh,
        in_specs=placed,
        out_specs=(P("pipe", "expert", None), P("pipe", "expert", None)),
        check_vma=False,
    )
```

profile of v0, /device:TPU:24, one launch (start us, length us, event | category | flops | bytes accessed | tf_op | source)
XLA Modules:
  0.0 452.3 jit_solution(4820935025356589106)
XLA Ops:
  1.9 1.9 convolution_convert_fusion.1
  3.7 2.9 broadcast_in_dim.32
  6.6 12.3 %all-to-all-start = ((bf16[64,4,7168]{2,1,0:T(4,128)(2,1)}), bf16[64,4,7168]{2,1,0:T(4,128)(2,1)}, u32[]{:S(2)}, u32[]{:S(2)}) async-start(bf16[64,4,7168]{2,1,0:T(4,128)(2,1)} %bitcast.65), calls=%async_computation | async-start | bytes 7340032 | tf_op jit(solution)/shard_map/all_to_all | solution.py:54
  21.0 82.5 %all-to-all-done = bf16[64,4,7168]{2,1,0:T(4,128)(2,1)} async-done(((bf16[64,4,7168]{2,1,0:T(4,128)(2,1)}), bf16[64,4,7168]{2,1,0:T(4,128)(2,1)}, u32[]{:S(2)}, u32[]{:S(2)}) %all-to-all-start) | async-done | bytes 3670048 | tf_op jit(solution)/shard_map/all_to_all | solution.py:54
  103.5 3.0 broadcast_in_dim.36
  106.5 6.0 %all-to-all-start.2 = ((bf16[64,4,7168]{2,1,0:T(4,128)(2,1)}), bf16[64,4,7168]{2,1,0:T(4,128)(2,1)}, u32[]{:S(2)}, u32[]{:S(2)}) async-start(bf16[64,4,7168]{2,1,0:T(4,128)(2,1)} %bitcast.66), calls=%async_computation.2 | async-start | bytes 7340032 | tf_op jit(solution)/shard_map/all_to_all | solution.py:72
  112.5 6.8 %reshape.65 = bf16[256,7168]{1,0:T(8,128)(2,1)} reshape(bf16[64,4,7168]{2,1,0:T(4,128)(2,1)} %all-to-all-done) | data formatting | bytes 7340032 | tf_op jit(solution)/shard_map/reshape | solution.py:56
  119.3 3.3 fusion.15
  124.2 72.9 %all-to-all-done.2 = bf16[64,4,7168]{2,1,0:T(4,128)(2,1)} async-done(((bf16[64,4,7168]{2,1,0:T(4,128)(2,1)}), bf16[64,4,7168]{2,1,0:T(4,128)(2,1)}, u32[]{:S(2)}, u32[]{:S(2)}) %all-to-all-start.2) | async-done | bytes 3670048 | tf_op jit(solution)/shard_map/all_to_all | solution.py:72
  197.1 6.7 %reshape.70 = bf16[256,7168]{1,0:T(8,128)(2,1)} reshape(bf16[64,4,7168]{2,1,0:T(4,128)(2,1)} %all-to-all-done.2) | data formatting | bytes 7340032 | tf_op jit(solution)/shard_map/reshape | solution.py:75
  203.8 3.7 fusion.7
  209.0 2.9 fusion
  212.0 7.0 %reshape.71 = bf16[64,4,7168]{2,1,0:T(4,128)(2,1)} reshape(bf16[256,7168]{1,0:T(8,128)(2,1)} %fusion) | data formatting | bytes 7340032 | tf_op jit(solution)/shard_map/reshape | solution.py:85
  219.0 6.4 %all-to-all-start.3 = ((bf16[64,4,7168]{2,1,0:T(4,128)(2,1)}), bf16[64,4,7168]{2,1,0:T(4,128)(2,1)}, u32[]{:S(2)}, u32[]{:S(2)}) async-start(bf16[64,4,7168]{2,1,0:T(4,128)(2,1)} %reshape.71), calls=%async_computation.3 | async-start | bytes 7340032 | tf_op jit(solution)/shard_map/all_to_all | solution.py:84
  225.4 3.0 convolution_convert_fusion
  228.4 7.0 %reshape.66 = bf16[64,4,7168]{2,1,0:T(4,128)(2,1)} reshape(bf16[256,7168]{1,0:T(8,128)(2,1)} %convolution_convert_fusion) | data formatting | bytes 7340032 | tf_op jit(solution)/shard_map/reshape | solution.py:63
  235.4 74.5 %all-to-all-done.3 = bf16[64,4,7168]{2,1,0:T(4,128)(2,1)} async-done(((bf16[64,4,7168]{2,1,0:T(4,128)(2,1)}), bf16[64,4,7168]{2,1,0:T(4,128)(2,1)}, u32[]{:S(2)}, u32[]{:S(2)}) %all-to-all-start.3) | async-done | bytes 3670048 | tf_op jit(solution)/shard_map/all_to_all | solution.py:84
  309.9 6.0 %all-to-all-start.1 = ((bf16[64,4,7168]{2,1,0:T(4,128)(2,1)}), bf16[64,4,7168]{2,1,0:T(4,128)(2,1)}, u32[]{:S(2)}, u32[]{:S(2)}) async-start(bf16[64,4,7168]{2,1,0:T(4,128)(2,1)} %reshape.66), calls=%async_computation.1 | async-start | bytes 7340032 | tf_op jit(solution)/shard_map/all_to_all | solution.py:64
  315.9 3.6 convert_reduce_fusion
  319.6 3.0 fusion.3
  323.3 77.1 %all-to-all-done.1 = bf16[64,4,7168]{2,1,0:T(4,128)(2,1)} async-done(((bf16[64,4,7168]{2,1,0:T(4,128)(2,1)}), bf16[64,4,7168]{2,1,0:T(4,128)(2,1)}, u32[]{:S(2)}, u32[]{:S(2)}) %all-to-all-start.1) | async-done | bytes 3670048 | tf_op jit(solution)/shard_map/all_to_all | solution.py:64
  400.5 3.6 convert_reduce_fusion.1
  406.3 41.8 %collective-permute-done = bf16[1,128,7168]{2,1,0:T(8,128)(2,1)S(1)} collective-permute-done((bf16[1,128,7168]{2,1,0:T(8,128)(2,1)S(1)}, bf16[1,128,7168]{2,1,0:T(8,128)(2,1)S(1)}, u32[]{:S(2)}, u32[]{:S(2)}) %collective-permute-start) | collective-permute-done | bytes 1835040 | tf_op jit(solution)/shard_map/ppermute | solution.py:13
  449.4 2.8 copy.45
  (36 shorter events, 10.5 us)
Async XLA Ops:
  0.6 118.7 %copy-start = (bf16[1,7168,128]{2,1,0:T(8,128)(2,1)S(1)}, bf16[1,7168,128]{2,1,0:T(8,128)(2,1)}, u32[]{:S(2)}) copy-start(bf16[1,7168,128]{2,1,0:T(8,128)(2,1)} %param.11) | copy-start | bytes 5505028
  6.6 12.3 %copy-start.6 = (s32[1,128,8]{1,2,0:T(8,128)S(1)}, s32[1,128,8]{1,2,0:T(8,128)}, u32[]{:S(2)}) copy-start(s32[1,128,8]{1,2,0:T(8,128)} %param.10) | copy-start | bytes 12292
  6.6 12.3 %copy-start.7 = (s32[1,128,8]{1,2,0:T(8,128)S(1)}, s32[1,128,8]{1,2,0:T(8,128)}, u32[]{:S(2)}) copy-start(s32[1,128,8]{1,2,0:T(8,128)} %param.9) | copy-start | bytes 12292
  6.6 96.8 %all-to-all-start = ((bf16[64,4,7168]{2,1,0:T(4,128)(2,1)}), bf16[64,4,7168]{2,1,0:T(4,128)(2,1)}, u32[]{:S(2)}, u32[]{:S(2)}) async-start(bf16[64,4,7168]{2,1,0:T(4,128)(2,1)} %bitcast.65), calls=%async_computation | async-start | bytes 7340032 | tf_op jit(solution)/shard_map/all_to_all | solution.py:54
  106.5 90.6 %all-to-all-start.2 = ((bf16[64,4,7168]{2,1,0:T(4,128)(2,1)}), bf16[64,4,7168]{2,1,0:T(4,128)(2,1)}, u32[]{:S(2)}, u32[]{:S(2)}) async-start(bf16[64,4,7168]{2,1,0:T(4,128)(2,1)} %bitcast.66), calls=%async_computation.2 | async-start | bytes 7340032 | tf_op jit(solution)/shard_map/all_to_all | solution.py:72
  119.3 3.3 copy-start.2
  119.3 3.7 copy-start.3
  207.5 1.5 copy-start.4
  219.0 6.4 %copy-start.5 = (bf16[1,128,7168]{2,1,0:T(8,128)(2,1)S(1)}, bf16[1,128,7168]{2,1,0:T(8,128)(2,1)}, u32[]{:S(2)}) copy-start(bf16[1,128,7168]{2,1,0:T(8,128)(2,1)} %param.13) | copy-start | bytes 5505028
  219.0 90.9 %all-to-all-start.3 = ((bf16[64,4,7168]{2,1,0:T(4,128)(2,1)}), bf16[64,4,7168]{2,1,0:T(4,128)(2,1)}, u32[]{:S(2)}, u32[]{:S(2)}) async-start(bf16[64,4,7168]{2,1,0:T(4,128)(2,1)} %reshape.71), calls=%async_computation.3 | async-start | bytes 7340032 | tf_op jit(solution)/shard_map/all_to_all | solution.py:84
  309.9 90.6 %all-to-all-start.1 = ((bf16[64,4,7168]{2,1,0:T(4,128)(2,1)}), bf16[64,4,7168]{2,1,0:T(4,128)(2,1)}, u32[]{:S(2)}, u32[]{:S(2)}) async-start(bf16[64,4,7168]{2,1,0:T(4,128)(2,1)} %reshape.66), calls=%async_computation.1 | async-start | bytes 7340032 | tf_op jit(solution)/shard_map/all_to_all | solution.py:64
  322.6 83.8 %collective-permute-start.1 = (bf16[1,128,7168]{2,1,0:T(8,128)(2,1)}, bf16[1,128,7168]{2,1,0:T(8,128)(2,1)}, u32[]{:S(2)}, u32[]{:S(2)}) collective-permute-start(bf16[1,128,7168]{2,1,0:T(8,128)(2,1)} %fusion.3), channel_id=1, source_target_pairs={{1,0},{2,1},{3,2},{0,3},{5,4},{6,5},{7,6},{4,7},{9,8},{10,9},{11,1... | collective-permute-start | bytes 5505032 | tf_op jit(solution)/shard_map/ppermute | solution.py:13
  406.0 42.1 %collective-permute-start = (bf16[1,128,7168]{2,1,0:T(8,128)(2,1)S(1)}, bf16[1,128,7168]{2,1,0:T(8,128)(2,1)S(1)}, u32[]{:S(2)}, u32[]{:S(2)}) collective-permute-start(bf16[1,128,7168]{2,1,0:T(8,128)(2,1)S(1)} %fusion.4), channel_id=1, source_target_pairs={{3,0},{0,1},{1,2},{2,3},{7,4},{4,5},{5,6},{6,7},{11,8},{8,9},{9,10... | collective-permute-start | bytes 5505032 | tf_op jit(solution)/shard_map/ppermute | solution.py:13
  448.2 4.1 copy-start.1
where the time goes:
time: 455 us; the launch traced here: 452 us
  waiting for transfers between devices  349 us (77%)
  local copies, waits for them, and re-layouts  38.5 us (8%)
  starting transfers between devices  31.8 us (7%)
  matrix products  23.9 us (5%)
  other arithmetic  8.52 us (2%)
    all_to_all x1, waiting for transfers between devices, on_device(): lax.all_to_all(spread_rows, 'expert', split_axis=0, concat_axis=0, tiled=...  82.5 us
    all_to_all x1, waiting for transfers between devices, on_device(): lax.all_to_all(return_partial_value, 'expert', split_axis=0, concat_axis=...  77.1 us
    all_to_all x1, waiting for transfers between devices, on_device(): lax.all_to_all(grad_part.reshape(devices, CAP, width), 'expert', split_ax...  74.5 us
    all_to_all x1, waiting for transfers between devices, on_device(): lax.all_to_all(spread_grads, 'expert', split_axis=0, concat_axis=0, tiled...  72.9 us
    ppermute x2, waiting for transfers between devices, from_behind(): return lax.ppermute(block, axis, route)  41.8 us
    all_to_all x1, starting transfers between devices, on_device(): lax.all_to_all(spread_rows, 'expert', split_axis=0, concat_axis=0, tiled=...  12.3 us
  transfers between devices with their start and end apart: 6, of which 5 were waited for; matrix products, arithmetic and copies ran while one was open for 8% of the time, Pallas kernels for 0%

commit v1 on v0

v1 whole, which is shorter than its diff:
```python
import jax
import jax.numpy as jnp
from jax import lax
from jax.sharding import PartitionSpec as P

FF = 2048
CAP = 4
FLIGHT = 4


def contract_rows(left, right):
    return lax.dot_general(
        left, right, (((1,), (1,)), ((), ())), preferred_element_type=jnp.float32
    )


def on_device(section_input, cotangent, routes, gate_codes, w_gate, w_up, w_down):
    highest = lax.Precision.HIGHEST
    tokens_in = section_input[0]
    grads_in = cotangent[0]
    route_ids = routes[0]
    codes_float = gate_codes[0].astype(jnp.float32)
    gate_cols = w_gate[0]
    up_cols = w_up[0]
    down_rows = w_down[0]
    devices = lax.axis_size("expert")
    group = devices // FLIGHT
    width = tokens_in.shape[1]
    across = [[f * group + i for f in range(FLIGHT)] for i in range(group)]
    along = [[f * group + i for i in range(group)] for f in range(FLIGHT)]
    route_weight = 2.5 * codes_float / jnp.sum(codes_float, axis=-1, keepdims=True)
    named = route_ids[:, :, None] == jnp.arange(FLIGHT, dtype=jnp.int32)
    matched = jnp.sum(named, axis=1)
    token_weight = jnp.sum(jnp.where(named, route_weight[:, :, None], 0.0), axis=1)
    position = jnp.cumsum(matched, axis=0) - 1
    selector = (matched.T[:, None, :] == 1) & (
        position.T[:, None, :] == jnp.arange(CAP, dtype=jnp.int32)[None, :, None]
    )
    slots = FLIGHT * CAP
    picks = selector.astype(jnp.bfloat16).reshape(slots, -1)
    picks_wide = selector.astype(jnp.float32)
    send_rows = jnp.dot(picks, tokens_in, preferred_element_type=jnp.float32).astype(jnp.bfloat16)
    slot_weight = jnp.einsum("fct,tf->fc", picks_wide, token_weight, precision=highest).reshape(slots)
    picks_wide = picks_wide.reshape(slots, -1)
    grad_slots = jnp.dot(picks, grads_in, preferred_element_type=jnp.float32)
    send_grads = (slot_weight[:, None] * grad_slots).astype(jnp.bfloat16)
    same = jnp.dot(picks_wide, picks_wide.T, precision=highest)
    earlier = jnp.tril(same, -1)
    first = (jnp.sum(earlier, axis=1) == 0).astype(jnp.float32)
    merge = first[:, None] * same
    place = (picks_wide * first[:, None]).astype(jnp.bfloat16)

    def gather(block):
        here = lax.all_to_all(
            block.reshape(FLIGHT, CAP, width), "expert", split_axis=0, concat_axis=0,
            axis_index_groups=across, tiled=True,
        )
        return lax.all_gather(
            here.reshape(slots, width), "expert", axis_index_groups=along, tiled=True
        )

    def reduce(block):
        here = lax.psum_scatter(
            block, "expert", scatter_dimension=0, axis_index_groups=along, tiled=True
        )
        return lax.all_to_all(
            here.reshape(FLIGHT, CAP, width), "expert", split_axis=0, concat_axis=0,
            axis_index_groups=across, tiled=True,
        ).reshape(slots, width)

    rows = gather(send_rows)
    gate = jnp.dot(rows, gate_cols, preferred_element_type=jnp.float32)
    upper = jnp.dot(rows, up_cols, preferred_element_type=jnp.float32)
    hidden = (jax.nn.silu(gate) * upper).astype(jnp.bfloat16)
    partial_value = jnp.dot(hidden, down_rows, preferred_element_type=jnp.float32).astype(
        jnp.bfloat16
    )
    grad_rows = gather(send_grads)
    out_sum = reduce(partial_value)
    d_hidden = contract_rows(grad_rows, down_rows)
    sigma = jax.nn.sigmoid(gate)
    d_gate = (d_hidden * upper * sigma * (1.0 + gate * (1.0 - sigma))).astype(jnp.bfloat16)
    d_up = (d_hidden * jax.nn.silu(gate)).astype(jnp.bfloat16)
    grad_part = (contract_rows(d_gate, gate_cols) + contract_rows(d_up, up_cols)).astype(
        jnp.bfloat16
    )
    grad_sum = reduce(grad_part)
    layer_out = jnp.dot(
        merge * slot_weight[None, :], out_sum.astype(jnp.float32), precision=highest
    ).astype(jnp.bfloat16)
    input_grad = jnp.dot(merge, grad_sum.astype(jnp.float32), precision=highest).astype(
        jnp.bfloat16
    )
    pipes = lax.axis_size("pipe")
    ahead = [(i, (i + 1) % pipes) for i in range(pipes)]
    back = [(i, (i - 1) % pipes) for i in range(pipes)]

    def spread(block, route):
        there = lax.ppermute(block, "pipe", route)
        where = lax.ppermute(place, "pipe", route)
        return lax.dot_general(
            where, there, (((0,), (0,)), ((), ())), preferred_element_type=jnp.float32
        ).astype(jnp.bfloat16)[None]

    return (spread(layer_out, ahead), spread(input_grad, back))


def solution(mesh):
    placed = (
        P("pipe", "expert", None),
        P("pipe", "expert", None),
        P("pipe", "expert", None),
        P("pipe", "expert", None),
        P("pipe", None, "expert"),
        P("pipe", None, "expert"),
        P("pipe", "expert", None),
    )
    return jax.shard_map(
        on_device,
        mesh=mesh,
        in_specs=placed,
        out_specs=(P("pipe", "expert", None), P("pipe", "expert", None)),
        check_vma=False,
    )
```

time: 455 us -> 268 us (0.59)
  waiting for transfers between devices: 349 us -> 188 us
  local copies, waits for them, and re-layouts: 38.5 us -> 6.37 us
  blocking collectives: 0 us -> 19.5 us
  starting transfers between devices: 31.8 us -> 13.4 us
  between operations: 0.78 us -> 13.9 us
  other arithmetic: 8.52 us -> 1.16 us
    all_to_all x4 -> x2, waiting for transfers between devices: 307 us -> 5.13 us  [reduce(): lax.all_to_all(here.reshape(FLIGHT, CAP, width), 'expert', split_axis=0,...]
    reduce_scatter x0 -> x2, waiting for transfers between devices: none -> 113 us  [reduce(): lax.psum_scatter(block, 'expert', scatter_dimension=0, axis_index_groups=...]
    all_gather x0 -> x2, waiting for transfers between devices: none -> 68.3 us  [gather(): lax.all_gather(here.reshape(slots, width), 'expert', axis_index_groups=al...]
    ppermute x2 -> x4, waiting for transfers between devices: 41.8 us -> 1.59 us  [the longest x2 1.58 us: spread(): where = lax.ppermute(place, 'pipe', route)]
    reshape x4 -> x8, local copies, waits for them, and re-layouts: 27.5 us -> 5.23 us  [the longest x2 3.43 us: reduce(): here.reshape(FLIGHT, CAP, width)]
    all_to_all x4 -> x2, starting transfers between devices: 30.7 us -> 8.49 us  [reduce(): lax.all_to_all(here.reshape(FLIGHT, CAP, width), 'expert', split_axis=0,...]
    all_to_all x0 -> x2, blocking collectives: none -> 19.5 us  [gather(): lax.all_to_all(block.reshape(FLIGHT, CAP, width), 'expert', split_axis=0,...]
    reduce_sum x2 -> x0, other arithmetic: 7.3 us -> none  [the longest x1 3.65 us: on_device(): jnp.sum(grad_back.astype(jnp.float32).reshape(flight, group, CAP, width),...]
  transfers between devices with their start and end apart: 6 -> 10, of which waited for: 5 -> 6; matrix products, arithmetic and copies ran while one was open for 8% -> 7% of each run, Pallas kernels for 0% -> 0%
where the time goes in v1:
time: 268 us; the launch traced here: 267 us
  waiting for transfers between devices  188 us (70%)
  matrix products  25.3 us (9%)
  blocking collectives  19.5 us (7%)
  between operations  13.9 us (5%)
  starting transfers between devices  13.4 us (5%)
  local copies, waits for them, and re-layouts  6.37 us (2%)
    reduce_scatter x2, waiting for transfers between devices, reduce(): lax.psum_scatter(block, 'expert', scatter_dimension=0, axis_index_groups=...  113 us
    all_gather x2, waiting for transfers between devices, gather(): lax.all_gather(here.reshape(slots, width), 'expert', axis_index_groups=al...  68.3 us
    all_to_all x2, blocking collectives, gather(): lax.all_to_all(block.reshape(FLIGHT, CAP, width), 'expert', split_axis=0,...  19.5 us
    all_to_all x2, starting transfers between devices, reduce(): lax.all_to_all(here.reshape(FLIGHT, CAP, width), 'expert', split_axis=0,...  8.49 us
    dot_general x3, matrix products, contract_rows(): lax.dot_general(left, right, (((1,), (1,)), ((), ())), preferred_element_...  7.81 us
  transfers between devices with their start and end apart: 10, of which 6 were waited for; matrix products, arithmetic and copies ran while one was open for 7% of the time, Pallas kernels for 0%

profile of v1, /device:TPU:24, one launch (start us, length us, event | category | flops | bytes accessed | tf_op | source)
XLA Modules:
  0.0 267.5 jit_solution(9766215268542456535)
XLA Ops:
  8.5 1.9 convolution_convert_fusion.5
  10.4 10.6 %all_to_all.20 = bf16[4,4,7168]{2,1,0:T(4,128)(2,1)S(1)} all-to-all(bf16[4,4,7168]{2,1,0:T(4,128)(2,1)S(1)} %reshape.176), channel_id=1, replica_groups={{0,64,128,192},{4,68,132,196},{8,72,136,200},{12,76,140,204},{16,80,144..., dimensions={0} | all-to-all | bytes 458752 | tf_op jit(solution)/shard_map/all_to_all | solution.py:54
  22.1 1.9 fusion.3
  24.1 8.9 %all_to_all.21 = bf16[4,4,7168]{2,1,0:T(4,128)(2,1)S(1)} all-to-all(bf16[4,4,7168]{2,1,0:T(4,128)(2,1)S(1)} %reshape.180), channel_id=1, replica_groups={{0,64,128,192},{4,68,132,196},{8,72,136,200},{12,76,140,204},{16,80,144..., dimensions={0} | all-to-all | bytes 458752 | tf_op jit(solution)/shard_map/all_to_all | solution.py:54
  33.8 30.6 %all-gather.3.cloned.1.call-done = bf16[256,7168]{1,0:T(8,128)(2,1)} async-done(((bf16[16,7168]{1,0:T(8,128)(2,1)}), bf16[256,7168]{1,0:T(8,128)(2,1)}) %all-gather.3.cloned.1.call-update) | async-done | bytes 3670032 | tf_op jit(solution)/shard_map/all_gather | solution.py:58
  64.4 3.3 %fusion.13 = f32[256,128]{1,0:T(8,128)S(1)} fusion(bf16[256,7168]{1,0:T(8,128)(2,1)} %all-gather.3.cloned.1.call-done, bf16[1,7168,128]{2,1,0:T(8,128)(2,1)S(1)} %copy-done), kind=kOutput, calls=%fused_computation.21 | convolution fusion | flops 469762048 | bytes 5636096 | tf_op jit(solution)/shard_map/dot_general | solution.py:72
  68.1 1.2 fusion.9
  69.3 37.7 %all-gather.5.cloned.1.call-done = bf16[256,7168]{1,0:T(8,128)(2,1)} async-done(((bf16[16,7168]{1,0:T(8,128)(2,1)}), bf16[256,7168]{1,0:T(8,128)(2,1)}) %all-gather.5.cloned.1.call-update) | async-done | bytes 3670032 | tf_op jit(solution)/shard_map/all_gather | solution.py:58
  107.0 3.7 %fusion.5 = f32[256,128]{1,0:T(8,128)S(1)} fusion(bf16[256,7168]{1,0:T(8,128)(2,1)} %all-gather.5.cloned.1.call-done, bf16[1,128,7168]{2,1,0:T(8,128)(2,1)} %param.13), kind=kOutput, calls=%fused_computation.13 | convolution fusion | flops 469762048 | bytes 5636096 | tf_op jit(solution)/shard_map/dot_general | solution.py:12
  110.8 1.1 fusion.11
  112.2 3.0 %fusion = bf16[256,7168]{1,0:T(8,128)(2,1)} fusion(f32[256,7168]{1,0:T(8,128)S(1)} %fusion.11, bf16[1,7168,128]{2,1,0:T(8,128)(2,1)S(1)} %copy-done.3, f32[256,128]{1,0:T(8,128)S(1)} %fusion.5, f32[256,128]{1,0:T(8,128)S(1)} %fusion.13), kind=kOutput, calls=%fused_computation.2 | convolution fusion | flops 473628672 | bytes 13107200 | tf_op jit(solution)/shard_map/dot_general | solution.py:12
  115.3 4.4 %convolution_convert_fusion = bf16[256,7168]{1,0:T(8,128)(2,1)} fusion(bf16[1,128,7168]{2,1,0:T(8,128)(2,1)} %param.13, f32[256,128]{1,0:T(8,128)S(1)} %fusion.9, f32[256,128]{1,0:T(8,128)S(1)} %fusion.13), kind=kOutput, calls=%fused_computation.1 | convolution fusion | flops 471793664 | bytes 5767168 | tf_op jit(solution)/shard_map/dot_general | solution.py:75
  120.0 55.9 %reduce-scatter.5.cloned.1.call-done = bf16[16,7168]{1,0:T(8,128)(2,1)} async-done(((bf16[256,7168]{1,0:T(8,128)(2,1)}), bf16[16,7168]{1,0:T(8,128)(2,1)}) %reduce-scatter.5.cloned.1.call-update) | async-done | bytes 229392 | tf_op jit(solution)/shard_map/reduce_scatter | solution.py:63
  175.9 1.7 reshape.182
  177.6 4.2 %all-to-all-start.3 = ((bf16[4,4,7168]{2,1,0:T(4,128)(2,1)}), bf16[4,4,7168]{2,1,0:T(4,128)(2,1)S(1)}, u32[]{:S(2)}, u32[]{:S(2)}) async-start(bf16[4,4,7168]{2,1,0:T(4,128)(2,1)} %reshape.182), calls=%async_computation.5 | async-start | bytes 458752 | tf_op jit(solution)/shard_map/all_to_all | solution.py:66
  181.8 56.8 %reduce-scatter.3.cloned.1.call-done = bf16[16,7168]{1,0:T(8,128)(2,1)} async-done(((bf16[256,7168]{1,0:T(8,128)(2,1)}), bf16[16,7168]{1,0:T(8,128)(2,1)}) %reduce-scatter.3.cloned.1.call-update) | async-done | bytes 229392 | tf_op jit(solution)/shard_map/reduce_scatter | solution.py:63
  238.7 1.7 reshape.178
  240.4 4.2 %all-to-all-start.1 = ((bf16[4,4,7168]{2,1,0:T(4,128)(2,1)}), bf16[4,4,7168]{2,1,0:T(4,128)(2,1)S(1)}, u32[]{:S(2)}, u32[]{:S(2)}) async-start(bf16[4,4,7168]{2,1,0:T(4,128)(2,1)} %reshape.178), calls=%async_computation.2 | async-start | bytes 458752 | tf_op jit(solution)/shard_map/all_to_all | solution.py:66
  246.0 5.1 %all-to-all-done.1 = bf16[4,4,7168]{2,1,0:T(4,128)(2,1)S(1)} async-done(((bf16[4,4,7168]{2,1,0:T(4,128)(2,1)}), bf16[4,4,7168]{2,1,0:T(4,128)(2,1)S(1)}, u32[]{:S(2)}, u32[]{:S(2)}) %all-to-all-start.1) | async-done | bytes 229408 | tf_op jit(solution)/shard_map/all_to_all | solution.py:66
  252.3 1.5 collective-permute-start.2
  253.9 1.7 collective-permute-start
  255.6 1.6 collective-permute-done.2
  257.2 1.9 fusion.2
  259.1 1.9 fusion.1
  (54 shorter events, 7.0 us)
Async XLA Ops:
  7.2 57.2 %copy-start = (bf16[1,7168,128]{2,1,0:T(8,128)(2,1)S(1)}, bf16[1,7168,128]{2,1,0:T(8,128)(2,1)}, u32[]{:S(2)}) copy-start(bf16[1,7168,128]{2,1,0:T(8,128)(2,1)} %param.11) | copy-start | bytes 5505028
  7.2 57.2 %all-gather.3.cloned.1.call-start = ((), (), s32[]{:S(2)}) async-start(), calls=%async_computation.6 | async-start | bytes 3899392 | tf_op jit(solution)/shard_map/all_gather | solution.py:58
  8.4 13.4 %copy-start.4 = (s32[1,128,8]{1,2,0:T(8,128)S(1)}, s32[1,128,8]{1,2,0:T(8,128)}, u32[]{:S(2)}) copy-start(s32[1,128,8]{1,2,0:T(8,128)} %param.10) | copy-start | bytes 12292
  8.5 13.4 %copy-start.5 = (s32[1,128,8]{1,2,0:T(8,128)S(1)}, s32[1,128,8]{1,2,0:T(8,128)}, u32[]{:S(2)}) copy-start(s32[1,128,8]{1,2,0:T(8,128)} %param.9) | copy-start | bytes 12292
  21.8 85.2 %all-gather.5.cloned.1.call-start = ((), (), s32[]{:S(2)}) async-start(), calls=%async_computation.8 | async-start | bytes 3899392 | tf_op jit(solution)/shard_map/all_gather | solution.py:58
  33.8 142.1 %reduce-scatter.5.cloned.1.call-start = ((), (), s32[]{:S(2)}) async-start(), calls=%async_computation.9 | async-start | bytes 3899392 | tf_op jit(solution)/shard_map/reduce_scatter | solution.py:63
  64.4 3.3 %copy-start.1 = (bf16[256,7168]{1,0:T(8,128)(2,1)S(1)}, bf16[256,7168]{1,0:T(8,128)(2,1)}, u32[]{:S(2)}) copy-start(bf16[256,7168]{1,0:T(8,128)(2,1)} %all-gather.3.cloned.1.call-done) | copy-start | bytes 11010052
  64.4 3.7 %copy-start.2 = (bf16[1,7168,128]{2,1,0:T(8,128)(2,1)S(1)}, bf16[1,7168,128]{2,1,0:T(8,128)(2,1)}, u32[]{:S(2)}) copy-start(bf16[1,7168,128]{2,1,0:T(8,128)(2,1)} %param.12) | copy-start | bytes 5505028
  110.7 1.5 copy-start.3
  115.2 123.4 %reduce-scatter.3.cloned.1.call-start = ((), (), s32[]{:S(2)}) async-start(), calls=%async_computation.7 | async-start | bytes 3899392 | tf_op jit(solution)/shard_map/reduce_scatter | solution.py:63
  177.6 62.8 %all-to-all-start.3 = ((bf16[4,4,7168]{2,1,0:T(4,128)(2,1)}), bf16[4,4,7168]{2,1,0:T(4,128)(2,1)S(1)}, u32[]{:S(2)}, u32[]{:S(2)}) async-start(bf16[4,4,7168]{2,1,0:T(4,128)(2,1)} %reshape.182), calls=%async_computation.5 | async-start | bytes 458752 | tf_op jit(solution)/shard_map/all_to_all | solution.py:66
  240.4 10.8 %all-to-all-start.1 = ((bf16[4,4,7168]{2,1,0:T(4,128)(2,1)}), bf16[4,4,7168]{2,1,0:T(4,128)(2,1)S(1)}, u32[]{:S(2)}, u32[]{:S(2)}) async-start(bf16[4,4,7168]{2,1,0:T(4,128)(2,1)} %reshape.178), calls=%async_computation.2 | async-start | bytes 458752 | tf_op jit(solution)/shard_map/all_to_all | solution.py:66
  245.1 12.1 %collective-permute-start.3 = (bf16[16,7168]{1,0:T(8,128)(2,1)S(1)}, bf16[16,7168]{1,0:T(8,128)(2,1)S(1)}, u32[]{:S(2)}, u32[]{:S(2)}) collective-permute-start(bf16[16,7168]{1,0:T(8,128)(2,1)S(1)} %convolution_convert_fusion.3), channel_id=1, source_target_pairs={{0,3},{1,0},{2,1},{3,2},{4,7},{5,4},{6,5},{7,6},{8,11},{9,8},{10,9... | collective-permute-start | bytes 688136 | tf_op jit(solution)/shard_map/ppermute | solution.py:99
  251.7 7.4 %collective-permute-start.1 = (bf16[16,7168]{1,0:T(8,128)(2,1)S(1)}, bf16[16,7168]{1,0:T(8,128)(2,1)S(1)}, u32[]{:S(2)}, u32[]{:S(2)}) collective-permute-start(bf16[16,7168]{1,0:T(8,128)(2,1)S(1)} %convolution_convert_fusion.4), channel_id=1, source_target_pairs={{0,1},{1,2},{2,3},{3,0},{4,5},{5,6},{6,7},{7,4},{8,9},{9,10},{10,1... | collective-permute-start | bytes 688136 | tf_op jit(solution)/shard_map/ppermute | solution.py:99
  252.3 4.8 %collective-permute-start.2 = (bf16[16,128]{1,0:T(8,128)(2,1)S(1)}, bf16[16,128]{1,0:T(8,128)(2,1)S(1)}, u32[]{:S(2)}, u32[]{:S(2)}) collective-permute-start(bf16[16,128]{1,0:T(8,128)(2,1)S(1)} %select_convert_fusion), channel_id=1, source_target_pairs={{0,3},{1,0},{2,1},{3,2},{4,7},{5,4},{6,5},{7,6},{8,11},{9,8},{10,9... | collective-permute-start | bytes 12296 | tf_op jit(solution)/shard_map/ppermute | solution.py:100
  253.9 5.2 %collective-permute-start = (bf16[16,128]{1,0:T(8,128)(2,1)S(1)}, bf16[16,128]{1,0:T(8,128)(2,1)S(1)}, u32[]{:S(2)}, u32[]{:S(2)}) collective-permute-start(bf16[16,128]{1,0:T(8,128)(2,1)S(1)} %select_convert_fusion), channel_id=1, source_target_pairs={{0,1},{1,2},{2,3},{3,0},{4,5},{5,6},{6,7},{7,4},{8,9},{9,10},{10,1... | collective-permute-start | bytes 12296 | tf_op jit(solution)/shard_map/ppermute | solution.py:100
Sparse Core Ops, SparseCore 0:
  21.9 42.4 all-gather.2
  66.8 40.1 all-gather.4
  115.4 60.4 reduce-scatter.4
  178.3 60.3 reduce-scatter.2

commit v2 on v0

v2 whole, which is shorter than its diff:
```python
import jax
import jax.numpy as jnp
from jax import lax
from jax.experimental import pallas as pl
from jax.experimental.pallas import tpu as pltpu
from jax.sharding import PartitionSpec as P

CAP = 4
FLIGHT = 4
SLOTS = FLIGHT * CAP
CORES = 2
QUARTERS = 4
RING = 8
HOPS = 7
TILE = 512
MESH = pl.DeviceIdType.MESH
F32 = jnp.float32
BF16 = jnp.bfloat16

RIGHT, LEFT = 0, 1
FROM = {RIGHT: (0, 1, 3, 5, 7), LEFT: (0, 2, 4, 6, 7)}
GATHER = {
    RIGHT: ((0, 0), (0, 1), (1, 0), (1, 1), (2, 0), (2, 1), (3, 0)),
    LEFT: ((0, 1), (0, 0), (1, 1), (1, 0), (2, 1), (2, 0), (3, 1)),
}
REDUCE = {
    LEFT: ((4, 0), (3, 1), (3, 0), (2, 1), (2, 0), (1, 1), (1, 0)),
    RIGHT: ((4, 1), (3, 0), (3, 1), (2, 0), (2, 1), (1, 0), (1, 1)),
}


def nt(left, right):
    return lax.dot_general(left, right, (((1,), (1,)), ((), ())), preferred_element_type=F32)


def tn(left, right):
    return lax.dot_general(left, right, (((0,), (0,)), ((), ())), preferred_element_type=F32)


def regroup(q):
    row = lax.broadcasted_iota(jnp.int32, (SLOTS, SLOTS * QUARTERS), 0)
    col = lax.broadcasted_iota(jnp.int32, (SLOTS, SLOTS * QUARTERS), 1)
    there = (row & ~3) * QUARTERS + (row & 3) + q * CAP
    return (col == there).astype(F32).astype(BF16)


def exchange(
    x_ref, g_ref, wy_ref, sel_ref, wg_ref, wu_ref, wd_ref,
    out_y, out_g, out_wy, out_sel,
    stage_x, stage_g, rows, grads, gu, wd, acc, a_gate, a_up, hid, dh, dgu,
    part_y, part_g, recv_y, recv_g, fin_y, fin_g,
    local_sems, w_send, w_recv, x_send, x_recv, s_send, s_recv,
    ring_send, ring_recv, fin_send, fin_recv,
):
    me = lax.axis_index("expert")
    y = lax.axis_index("pipe")
    pipes = lax.axis_size("pipe")
    core = lax.rem(me, CORES)
    z = lax.rem(lax.div(me, CORES), RING)
    x = lax.div(me, CORES * RING)
    width = wd.shape[1]
    half = width // 2
    quarter = width // QUARTERS
    units = wg_ref.shape[1]

    def at(xx, zz, cc, yy):
        return ((xx * RING + zz) * CORES + cc, yy)

    ahead = lax.rem(y + 1, pipes)
    behind = lax.rem(y + pipes - 1, pipes)
    sibling = at(x, z, 1 - core, y)
    next_on = {
        RIGHT: at(x, lax.rem(z + 1, RING), core, y),
        LEFT: at(x, lax.rem(z + RING - 1, RING), core, y),
    }
    across = [at(lax.rem(x + k, FLIGHT), z, core, y) for k in range(FLIGHT)]
    up = [at(lax.rem(x + k, FLIGHT), z, core, ahead) for k in range(FLIGHT)]
    down = [at(lax.rem(x + k, FLIGHT), z, core, behind) for k in range(FLIGHT)]

    own = [
        pltpu.make_async_copy(wg_ref, gu.at[:, pl.ds(0, units)], local_sems.at[0]),
        pltpu.make_async_copy(wu_ref, gu.at[:, pl.ds(2 * units, units)], local_sems.at[1]),
        pltpu.make_async_copy(wd_ref, wd.at[pl.ds(0, units)], local_sems.at[2]),
    ]
    for copy in own:
        copy.start()

    barrier = pltpu.get_barrier_semaphore()
    peers = [sibling, next_on[RIGHT], next_on[LEFT]] + across[1:] + up + down
    for peer in peers:
        pl.semaphore_signal(barrier, inc=1, device_id=peer, device_id_type=MESH)
    pl.semaphore_wait(barrier, len(peers))

    def remote(src, dst, send, recv, device):
        return pltpu.make_async_remote_copy(
            src_ref=src, dst_ref=dst, send_sem=send, recv_sem=recv,
            device_id=device, device_id_type=MESH,
        )

    x_copies = []
    for i, (src, stage) in enumerate(((x_ref, stage_x), (g_ref, stage_g))):
        x_copies.append([
            remote(src.at[lax.rem(x + k, FLIGHT)], stage.at[x], x_send.at[i, k], x_recv.at[i, k], across[k])
            for k in range(1, FLIGHT)
        ])
    for copy in x_copies[0] + x_copies[1]:
        copy.start()
    stage_x[x] = x_ref[x]
    stage_g[x] = g_ref[x]
    small = [
        remote(wy_ref, out_wy, s_send.at[0], s_recv.at[0], up[0]),
        remote(sel_ref, out_sel, s_send.at[1], s_recv.at[1], down[0]),
    ]
    other = [
        remote(wg_ref, gu.at[:, pl.ds(units, units)], w_send.at[0], w_recv.at[0], sibling),
        remote(wu_ref, gu.at[:, pl.ds(3 * units, units)], w_send.at[1], w_recv.at[1], sibling),
        remote(wd_ref, wd.at[pl.ds(units, units)], w_send.at[2], w_recv.at[2], sibling),
    ]
    for copy in other + small:
        copy.start()

    def natural(stage, dst):
        def body(i, carry):
            cols = pl.ds(pl.multiple_of(i * 256, 256), 256)
            block = stage[:, :, cols].reshape(SLOTS * QUARTERS, 256)
            for q in range(QUARTERS):
                got = jnp.dot(regroup(q), block, preferred_element_type=F32)
                dst[pl.ds(0, SLOTS), pl.ds(pl.multiple_of(q * quarter + i * 256, 256), 256)] = got.astype(BF16)
            return carry
        lax.fori_loop(0, quarter // 256, body, 0)

    def block_of(buf, place, h):
        return buf.at[pl.ds(SLOTS * place, SLOTS), pl.ds(half * h, half)]

    def gather_copy(kind, buf, way, k):
        distance, h = GATHER[way][k]
        return remote(
            block_of(buf, FROM[way][distance], h), block_of(buf, FROM[way][distance + 1], h),
            ring_send.at[kind, way, k], ring_recv.at[kind, way, k], next_on[way],
        )

    def gather_step(kind, buf, k):
        for way in (RIGHT, LEFT):
            if k >= 2:
                gather_copy(kind, buf, way, k - 2).wait_recv()
            gather_copy(kind, buf, way, k).start()

    def gather_end(kind, buf):
        for k in (HOPS - 2, HOPS - 1):
            for way in (RIGHT, LEFT):
                gather_copy(kind, buf, way, k).wait_recv()

    def reduce_copy(kind, part, recv, way, k):
        distance, h = REDUCE[way][k]
        return remote(
            block_of(part, FROM[1 - way][distance], h), recv.at[way, k],
            ring_send.at[kind, way, k], ring_recv.at[kind, way, k], next_on[way],
        )

    def reduce_step(kind, part, recv, k):
        for way in (RIGHT, LEFT):
            if k >= 2:
                reduce_copy(kind, part, recv, way, k - 2).wait_recv()
                distance, h = REDUCE[way][k]
                place = FROM[1 - way][distance]
                rs, cs = pl.ds(SLOTS * place, SLOTS), pl.ds(half * h, half)
                part[rs, cs] = (part[rs, cs].astype(F32) + recv[way, k - 2].astype(F32)).astype(BF16)
            reduce_copy(kind, part, recv, way, k).start()

    def finish(kind, part, recv, fin, out, targets, i):
        for k in (HOPS - 2, HOPS - 1):
            for way in (RIGHT, LEFT):
                reduce_copy(kind, part, recv, way, k).wait_recv()
        for h in range(2):
            from_left = HOPS - 2 if REDUCE[LEFT][HOPS - 2][1] == h else HOPS - 1
            from_right = HOPS - 2 if REDUCE[RIGHT][HOPS - 2][1] == h else HOPS - 1
            rs, cs = pl.ds(0, SLOTS), pl.ds(half * h, half)
            total = part[rs, cs].astype(F32) + recv[LEFT, from_left].astype(F32)
            part[rs, cs] = (total + recv[RIGHT, from_right].astype(F32)).astype(BF16)

        def body(j, carry):
            cols = pl.ds(pl.multiple_of(j * 256, 256), 256)
            got = jnp.zeros((SLOTS * QUARTERS, 256), F32)
            for q in range(QUARTERS):
                block = part[pl.ds(0, SLOTS), pl.ds(pl.multiple_of(q * quarter + j * 256, 256), 256)]
                got += tn(regroup(q), block)
            fin[:, :, cols] = got.astype(BF16).reshape(FLIGHT, SLOTS, 256)
            return carry
        lax.fori_loop(0, quarter // 256, body, 0)
        copies = [
            remote(fin.at[lax.rem(x + k, FLIGHT)], out.at[x], fin_send.at[i, k], fin_recv.at[i, k], targets[k])
            for k in range(FLIGHT)
        ]
        for copy in copies:
            copy.start()
        return copies

    def gate_up(first, last):
        def body(i, carry):
            ks = pl.ds(pl.multiple_of(i * TILE, TILE), TILE)
            acc[...] += jnp.dot(rows[:, ks], gu[ks, :], preferred_element_type=F32)
            return carry
        lax.fori_loop(first, last, body, 0)

    def activate():
        gate, upper = acc[:, : 2 * units], acc[:, 2 * units :]
        sigma = jax.nn.sigmoid(gate)
        silu = gate * sigma
        hid[...] = (silu * upper).astype(BF16)
        a_gate[...] = upper * sigma * (1.0 + gate * (1.0 - sigma))
        a_up[...] = silu

    def outputs(first, last):
        def body(i, carry):
            cols = pl.ds(pl.multiple_of(i * TILE, TILE), TILE)
            part_y[:, cols] = jnp.dot(hid[...], wd[:, cols], preferred_element_type=F32).astype(BF16)
            return carry
        lax.fori_loop(first, last, body, 0)

    def d_hidden(first, last):
        def body(i, carry):
            ks = pl.ds(pl.multiple_of(i * TILE, TILE), TILE)
            dh[...] += nt(grads[:, ks], wd[:, ks])
            return carry
        lax.fori_loop(first, last, body, 0)

    def d_inputs(first, last):
        def body(i, carry):
            cols = pl.ds(pl.multiple_of(i * TILE, TILE), TILE)
            part_g[:, cols] = nt(dgu[...], gu[cols, :]).astype(BF16)
            return carry
        lax.fori_loop(first, last, body, 0)

    tiles = width // TILE

    for copy in x_copies[0]:
        copy.wait_recv()
    natural(stage_x, rows)
    gather_step(0, rows, 0)
    gather_step(0, rows, 1)
    for copy in x_copies[1]:
        copy.wait_recv()
    natural(stage_g, grads)
    acc[...] = jnp.zeros_like(acc)
    dh[...] = jnp.zeros_like(dh)
    for k in range(2, HOPS):
        gather_step(0, rows, k)

    gather_step(1, grads, 0)
    gather_step(1, grads, 1)
    gather_end(0, rows)
    for copy in own:
        copy.wait()
    for copy in other:
        copy.wait_recv()
    gate_up(0, tiles // 2)
    gather_step(1, grads, 2)
    gate_up(tiles // 2, tiles)
    gather_step(1, grads, 3)
    activate()
    outputs(0, tiles // 2)
    gather_step(1, grads, 4)
    outputs(tiles // 2, tiles)
    gather_step(1, grads, 5)
    gather_step(1, grads, 6)

    reduce_step(2, part_y, recv_y, 0)
    reduce_step(2, part_y, recv_y, 1)
    gather_end(1, grads)
    d_hidden(0, tiles)
    reduce_step(2, part_y, recv_y, 2)
    dgu[:, : 2 * units] = (dh[...] * a_gate[...]).astype(BF16)
    dgu[:, 2 * units :] = (dh[...] * a_up[...]).astype(BF16)
    d_inputs(0, tiles // 2)
    reduce_step(2, part_y, recv_y, 3)
    d_inputs(tiles // 2, tiles)
    for k in range(4, HOPS):
        reduce_step(2, part_y, recv_y, k)

    reduce_step(3, part_g, recv_g, 0)
    reduce_step(3, part_g, recv_g, 1)
    done = finish(2, part_y, recv_y, fin_y, out_y, up, 0)
    for k in range(2, HOPS):
        reduce_step(3, part_g, recv_g, k)
    done += finish(3, part_g, recv_g, fin_g, out_g, down, 1)

    for copy in x_copies[0] + x_copies[1] + other:
        copy.wait_send()
    for copy in small + done:
        copy.wait()
    for k in range(HOPS):
        for way in (RIGHT, LEFT):
            gather_copy(0, rows, way, k).wait_send()
            gather_copy(1, grads, way, k).wait_send()
            reduce_copy(2, part_y, recv_y, way, k).wait_send()
            reduce_copy(3, part_g, recv_g, way, k).wait_send()


def place_kernel(y_ref, g_ref, wy_ref, sel_ref, out_ref, grad_ref):
    q = pl.program_id(0)
    row = lax.broadcasted_iota(jnp.int32, wy_ref.shape, 0)
    mine = ((row // CAP) & (QUARTERS - 1)) == q
    weight = jnp.where(mine, wy_ref[...], 0.0)
    high = weight.astype(BF16)
    rest = weight - high.astype(F32)
    mid = rest.astype(BF16)
    low = (rest - mid.astype(F32)).astype(BF16)
    block = y_ref[...].reshape(SLOTS * QUARTERS, -1)
    total = tn(jnp.concatenate([high, mid, low], axis=0), jnp.concatenate([block] * 3, axis=0))
    out_ref[...] = total.astype(BF16)
    pick = jnp.where(mine, sel_ref[...], 0.0).astype(BF16)
    grad_ref[...] = tn(pick, g_ref[...].reshape(SLOTS * QUARTERS, -1)).astype(BF16)


def on_device(section_input, cotangent, routes, gate_codes, w_gate, w_up, w_down):
    highest = lax.Precision.HIGHEST
    tokens_in = section_input[0]
    grads_in = cotangent[0]
    route_ids = routes[0]
    codes_float = gate_codes[0].astype(F32)
    tokens, width = tokens_in.shape
    quarter = width // QUARTERS
    half = width // 2
    units = w_gate.shape[2]
    route_weight = 2.5 * codes_float / jnp.sum(codes_float, axis=-1, keepdims=True)
    named = route_ids[:, :, None] == jnp.arange(FLIGHT, dtype=jnp.int32)
    matched = jnp.sum(named, axis=1)
    token_weight = jnp.sum(jnp.where(named, route_weight[:, :, None], 0.0), axis=1)
    position = jnp.cumsum(matched, axis=0) - 1
    selector = (matched.T[:, None, None, :] == 1) & (
        position.T[:, None, None, :] == jnp.arange(CAP, dtype=jnp.int32)[None, None, :, None]
    )
    selector = jnp.broadcast_to(selector, (FLIGHT, QUARTERS, CAP, tokens))
    which = jnp.arange(QUARTERS)[None, :, None, None]
    sel64 = selector.astype(F32).reshape(-1, tokens)
    wy64 = jnp.where(selector, token_weight.T[:, None, None, :], 0.0).reshape(-1, tokens)
    slot_weight = jnp.sum(wy64, axis=1, keepdims=True)

    def choose(block):
        total = 0.0
        for q in range(QUARTERS):
            picks = (selector & (which == q)).astype(BF16).reshape(-1, tokens)
            total += jnp.dot(
                picks, block[:, q * quarter : (q + 1) * quarter], preferred_element_type=F32
            )
        return total

    send_rows = choose(tokens_in).astype(BF16).reshape(FLIGHT, SLOTS, quarter)
    send_grads = (slot_weight * choose(grads_in)).astype(BF16).reshape(FLIGHT, SLOTS, quarter)

    vmem = pl.BlockSpec(memory_space=pltpu.VMEM)
    hbm = pl.BlockSpec(memory_space=pl.ANY)
    blocks = FLIGHT, SLOTS, quarter
    count = RING * SLOTS
    dma = pltpu.SemaphoreType.DMA
    got_y, got_g, got_wy, got_sel = pl.pallas_call(
        exchange,
        out_shape=(
            jax.ShapeDtypeStruct(blocks, BF16),
            jax.ShapeDtypeStruct(blocks, BF16),
            jax.ShapeDtypeStruct(wy64.shape, F32),
            jax.ShapeDtypeStruct(sel64.shape, F32),
        ),
        in_specs=[vmem] * 4 + [hbm] * 3,
        out_specs=(vmem,) * 4,
        scratch_shapes=[
            pltpu.VMEM(blocks, BF16),
            pltpu.VMEM(blocks, BF16),
            pltpu.VMEM((count, width), BF16),
            pltpu.VMEM((count, width), BF16),
            pltpu.VMEM((width, 4 * units), BF16),
            pltpu.VMEM((2 * units, width), BF16),
            pltpu.VMEM((count, 4 * units), F32),
            pltpu.VMEM((count, 2 * units), F32),
            pltpu.VMEM((count, 2 * units), F32),
            pltpu.VMEM((count, 2 * units), BF16),
            pltpu.VMEM((count, 2 * units), F32),
            pltpu.VMEM((count, 4 * units), BF16),
            pltpu.VMEM((count, width), BF16),
            pltpu.VMEM((count, width), BF16),
            pltpu.VMEM((2, HOPS, SLOTS, half), BF16),
            pltpu.VMEM((2, HOPS, SLOTS, half), BF16),
            pltpu.VMEM(blocks, BF16),
            pltpu.VMEM(blocks, BF16),
            dma((3,)),
            dma((3,)),
            dma((3,)),
            dma((2, FLIGHT)),
            dma((2, FLIGHT)),
            dma((2,)),
            dma((2,)),
            dma((4, 2, HOPS)),
            dma((4, 2, HOPS)),
            dma((2, FLIGHT)),
            dma((2, FLIGHT)),
        ],
        compiler_params=pltpu.CompilerParams(
            collective_id=0, has_side_effects=True, vmem_limit_bytes=48 * 2**20
        ),
        cost_estimate=pl.CostEstimate(
            flops=12 * count * width * units * 2, bytes_accessed=6 * units * width, transcendentals=0
        ),
        name="exchange",
    )(send_rows, send_grads, wy64, sel64, w_gate[0], w_up[0], w_down[0])

    whole = lambda shape: pl.BlockSpec(shape, lambda q: (0,) * len(shape))
    column = pl.BlockSpec((tokens, quarter), lambda q: (0, q))
    passed, grad_passed = pl.pallas_call(
        place_kernel,
        grid=(QUARTERS,),
        out_shape=(jax.ShapeDtypeStruct((tokens, width), BF16),) * 2,
        in_specs=[whole(blocks), whole(blocks), whole(wy64.shape), whole(sel64.shape)],
        out_specs=(column, column),
        name="place",
    )(got_y, got_g, got_wy, got_sel)
    return passed[None], grad_passed[None]


def solution(mesh):
    placed = (
        P("pipe", "expert", None),
        P("pipe", "expert", None),
        P("pipe", "expert", None),
        P("pipe", "expert", None),
        P("pipe", None, "expert"),
        P("pipe", None, "expert"),
        P("pipe", "expert", None),
    )
    return jax.shard_map(
        on_device,
        mesh=mesh,
        in_specs=placed,
        out_specs=(P("pipe", "expert", None), P("pipe", "expert", None)),
        check_vma=False,
    )
```

time: 455 us -> 115 us (0.25)
  waiting for transfers between devices: 349 us -> 0 us
  Pallas kernels: 0 us -> 101 us
  local copies, waits for them, and re-layouts: 38.5 us -> 4.79 us
  starting transfers between devices: 31.8 us -> 0 us
  matrix products: 23.9 us -> 4.26 us
  other arithmetic: 8.52 us -> 3.28 us
    all_to_all x4 -> x0, waiting for transfers between devices: 307 us -> none  [the longest x1 82.5 us: on_device(): lax.all_to_all(spread_rows, 'expert', split_axis=0, concat_axis=0, tiled=...]
    pallas_call x0 -> x2, Pallas kernels: none -> 101 us  [the longest x1 97.2 us: on_device(): pl.pallas_call(exchange, out_shape=(jax.ShapeDtypeStruct(blocks, BF16), j...]
    ppermute x2 -> x0, waiting for transfers between devices: 41.8 us -> none  [from_behind(): return lax.ppermute(block, axis, route)]
    all_to_all x4 -> x0, starting transfers between devices: 30.7 us -> none  [the longest x1 12.3 us: on_device(): lax.all_to_all(spread_rows, 'expert', split_axis=0, concat_axis=0, tiled=...]
    reshape x4 -> x0, local copies, waits for them, and re-layouts: 27.5 us -> none  [the longest x1 7.02 us: on_device(): grad_part.reshape(devices, CAP, width)]
    dot_general x11 -> x8, matrix products: 23.9 us -> 4.26 us  [choose(): jnp.dot(picks, block[:, q * quarter:(q + 1) * quarter], preferred_element...]
    reduce_sum x2 -> x1, other arithmetic: 7.3 us -> 0.1 us  [on_device(): slot_weight = jnp.sum(wy64, axis=1, keepdims=True)]
    broadcast_in_dim x2 -> x3, local copies, waits for them, and re-layouts: 5.91 us -> 0.02 us  [the longest x2 0.01 us: on_device(): selector = jnp.broadcast_to(selector, (FLIGHT, QUARTERS, CAP, tokens))]
  transfers between devices with their start and end apart: 6 -> 0, of which waited for: 5 -> 0; matrix products, arithmetic and copies ran while one was open for 8% -> 0% of each run, Pallas kernels for 0% -> 0%
where the time goes in v2:
time: 115 us; the launch traced here: 114 us
  Pallas kernels  101 us (88%)
  local copies, waits for them, and re-layouts  4.79 us (4%)
  matrix products  4.26 us (4%)
  other arithmetic  3.28 us (3%)
    pallas_call x1, Pallas kernels, on_device(): pl.pallas_call(exchange, out_shape=(jax.ShapeDtypeStruct(blocks, BF16), j...  97.2 us
    dot_general x8, matrix products, choose(): jnp.dot(picks, block[:, q * quarter:(q + 1) * quarter], preferred_element...  4.26 us
    pallas_call x1, Pallas kernels, on_device(): pl.pallas_call(place_kernel, grid=(QUARTERS,), out_shape=(jax.ShapeDtypeS...  4.05 us
    unnamed x16, local copies, waits for them, and re-layouts  3.81 us

profile of v2, /device:TPU:24, one launch (start us, length us, event | category | flops | bytes accessed | tf_op | source)
XLA Modules:
  0.0 114.4 jit_solution(13865122172891975537)
XLA Ops:
  0.6 0.8 convert_reduce_fusion.1
  1.8 0.1 and.92
  2.2 0.7 convert_reduce_fusion
  2.9 0.7 bitcast_divide_fusion
  3.6 0.7 select_reduce_fusion.1
  4.3 0.1 copy.13
  4.5 0.2 reduce_window_sum.11
  4.7 0.1 select_reduce_fusion
  5.0 1.3 %fusion.6 = f32[64,1792]{1,0:T(8,128)S(1)} fusion(bf16[128,7168]{1,0:T(8,128)(2,1)} %bitcast.25, pred[64,128]{1,0:T(8,128)(4,1)S(1)} %bitcast.34, pred[64]{0:T(512)(128)(4,1)S(1)} %and.84), kind=kOutput, calls=%fused_computation.12 | convolution fusion | flops 29368320 | bytes 925760 | tf_op jit(solution)/shard_map/dot_general | solution.py:343
  6.3 1.4 %convolution_add_fusion.2 = f32[64,1792]{1,0:T(8,128)S(1)} fusion(f32[64,1792]{1,0:T(8,128)S(1)} %fusion.6, bf16[128,7168]{1,0:T(8,128)(2,1)} %bitcast.26, pred[64,128]{1,0:T(8,128)(4,1)S(1)} %bitcast.35, pred[64]{0:T(512)(128)(4,1)S(1)} %and.88), kind=kOutput, calls=%fused_computation.3 | convolution fusion | flops 29483008 | bytes 1384512 | tf_op jit(solution)/shard_map/dot_general | solution.py:343
  7.7 0.3 convolution_add_fusion.1
  8.0 0.3 fusion.2
  8.3 0.3 fusion.11
  8.5 0.3 convolution_add_fusion.5
  8.8 0.3 convolution_add_fusion.4
  9.1 0.3 fusion.1
  9.4 0.7 copy-done.4
  10.0 0.6 copy-done.5
  10.6 97.2 %exchange.1 = (bf16[4,16,1792]{2,1,0:T(8,128)(2,1)S(1)}, bf16[4,16,1792]{2,1,0:T(8,128)(2,1)S(1)}, f32[64,128]{1,0:T(8,128)S(1)}, f32[64,128]{1,0:T(8,128)S(1)}) custom-call(bf16[4,16,1792]{2,1,0:T(8,128)(2,1)S(1)} %bitcast.21, bf16[4,16,1792]{2,1,0:T(8,128)(2,1)S(1)} %bitcast.20, f32[64,128]{1,0:T(8,128)S(1)} %broadcast_select_fusion.wy_ref, ...), custom_call_target="tpu_custom_call" | custom-call | flops 2818572288 | bytes 5505024 | tf_op jit(solution)/shard_map/exchange/pallas_call | solution.py:356
  107.8 0.7 copy-done
  108.5 0.7 copy-done.1
  109.2 0.6 copy-done.2
  109.8 0.6 copy-done.3
  110.4 4.1 %place.1 = (bf16[128,7168]{1,0:T(8,128)(2,1)}, bf16[128,7168]{1,0:T(8,128)(2,1)}) custom-call(bf16[4,16,1792]{2,1,0:T(8,128)(2,1)} %copy-done, bf16[4,16,1792]{2,1,0:T(8,128)(2,1)} %copy-done.1, f32[64,128]{1,0:T(8,128)} %copy-done.2, f32[64,128]{1,0:T(8,128)} %copy-done.3), custom_call_target="tpu_custom_call" | custom-call | tf_op jit(solution)/shard_map/place/pallas_call | solution.py:408
  (30 shorter events, 0.9 us)
Async XLA Ops:
  0.6 7.1 %copy-start.6 = (bf16[1,128,7168]{2,1,0:T(8,128)(2,1)S(1)}, bf16[1,128,7168]{2,1,0:T(8,128)(2,1)}, u32[]{:S(2)}) copy-start(bf16[1,128,7168]{2,1,0:T(8,128)(2,1)} %param.8) | copy-start | bytes 5505028
  6.3 2.0 %copy-start.7 = (bf16[1,128,7168]{2,1,0:T(8,128)(2,1)S(1)}, bf16[1,128,7168]{2,1,0:T(8,128)(2,1)}, u32[]{:S(2)}) copy-start(bf16[1,128,7168]{2,1,0:T(8,128)(2,1)} %param.7) | copy-start | bytes 5505028
  8.5 1.5 %copy-start.4 = (bf16[1,7168,128]{2,1,0:T(8,128)(2,1)S(1)}, bf16[1,7168,128]{2,1,0:T(8,128)(2,1)}, u32[]{:S(2)}) copy-start(bf16[1,7168,128]{2,1,0:T(8,128)(2,1)} %param.11) | copy-start | bytes 5505028
  8.5 2.0 %copy-start.5 = (bf16[1,7168,128]{2,1,0:T(8,128)(2,1)S(1)}, bf16[1,7168,128]{2,1,0:T(8,128)(2,1)}, u32[]{:S(2)}) copy-start(bf16[1,7168,128]{2,1,0:T(8,128)(2,1)} %param.12) | copy-start | bytes 5505028
  107.8 0.7 copy-start
  108.5 0.7 copy-start.1
  109.2 0.6 copy-start.2
  109.8 0.6 copy-start.3

commit v3 on v0

v3 whole, which is shorter than its diff:
```python
import jax
import jax.numpy as jnp
from jax import lax
from jax.experimental import pallas as pl
from jax.experimental.pallas import tpu as pltpu
from jax.sharding import PartitionSpec as P

CAP = 4
FLIGHT = 4
QUARTERS = 4
CORES = 2
RING = 8
UNIT = QUARTERS * CAP
STACK = FLIGHT * UNIT
COLS = 256
TILE = 512
MESH = pl.DeviceIdType.MESH
F32 = jnp.float32
BF16 = jnp.bfloat16

RIGHT, LEFT = 0, 1
WAYS = (RIGHT, LEFT)
FROM = {RIGHT: (0, 1, 3, 5, 7), LEFT: (0, 2, 4, 6, 7)}
ROWS = {
    RIGHT: ((0, 0, 1), (0, 1, 1), (0, 2, 1), (0, 3, 1), (1, 0, 2), (1, 2, 2), (2, 0, 2), (2, 2, 2), (3, 0, 2)),
    LEFT: ((0, 0, 1), (0, 3, 1), (0, 2, 1), (0, 1, 1), (1, 2, 2), (1, 0, 2), (2, 2, 2), (2, 0, 2), (3, 2, 2)),
}
GRADS = {
    RIGHT: ((0, 0, 2), (0, 2, 2), (1, 0, 2), (1, 2, 2), (2, 0, 2), (2, 2, 2), (3, 0, 2)),
    LEFT: ((0, 2, 2), (0, 0, 2), (1, 2, 2), (1, 0, 2), (2, 2, 2), (2, 0, 2), (3, 2, 2)),
}
SUMS = {
    LEFT: ((4, 0), (3, 2), (3, 0), (2, 2), (2, 0), (1, 2), (1, 0)),
    RIGHT: ((4, 2), (3, 0), (3, 2), (2, 0), (2, 2), (1, 0), (1, 2)),
}
STEPS = len(SUMS[LEFT])


def nt(left, right):
    return lax.dot_general(left, right, (((1,), (1,)), ((), ())), preferred_element_type=F32)


def tn(left, right):
    return lax.dot_general(left, right, (((0,), (0,)), ((), ())), preferred_element_type=F32)


def dot(left, right):
    return jnp.dot(left, right, preferred_element_type=F32)


def iota(shape, dim):
    return lax.broadcasted_iota(jnp.int32, shape, dim)


def exchange(
    routes_ref, codes_ref, tok_hbm, cot_hbm, wg_ref, wu_ref, wd_ref,
    out_ref, grad_ref,
    tok, cot, pick_x, pick_g, rows, grads, nat, gu, wd, swap, acc, a_gate, a_up, hid, dh, dgu,
    part_y, part_g, recv_y, recv_g, got_y, got_g, sel, wsel, sel_in, wsel_in,
    local_sems, w_send, w_recv, x_send, x_recv, s_send, s_recv,
    ring_send, ring_recv, fin_send, fin_recv,
):
    me = lax.axis_index("expert")
    y = lax.axis_index("pipe")
    pipes = lax.axis_size("pipe")
    core = lax.rem(me, CORES)
    z = lax.rem(lax.div(me, CORES), RING)
    x = lax.div(me, CORES * RING)
    tokens, width = tok.shape
    quarter = width // QUARTERS
    units = wg_ref.shape[1]
    count = nat.shape[0]

    def at(xx, zz, cc, yy):
        return ((xx * RING + zz) * CORES + cc, yy)

    ahead = lax.rem(y + 1, pipes)
    behind = lax.rem(y + pipes - 1, pipes)
    sibling = at(x, z, 1 - core, y)
    next_on = {
        RIGHT: at(x, lax.rem(z + 1, RING), core, y),
        LEFT: at(x, lax.rem(z + RING - 1, RING), core, y),
    }
    plane = [lax.rem(x + k, FLIGHT) for k in range(FLIGHT)]
    across = [at(xx, z, core, y) for xx in plane]
    up = [at(xx, z, core, ahead) for xx in plane]
    down = [at(xx, z, core, behind) for xx in plane]

    barrier = pltpu.get_barrier_semaphore()
    peers = [sibling, next_on[RIGHT], next_on[LEFT]] + across[1:] + up + down
    for peer in peers:
        pl.semaphore_signal(barrier, inc=1, device_id=peer, device_id_type=MESH)

    own = [
        pltpu.make_async_copy(tok_hbm, tok, local_sems.at[0]),
        pltpu.make_async_copy(cot_hbm, cot, local_sems.at[1]),
        pltpu.make_async_copy(wg_ref, gu.at[:, pl.ds(0, units)], local_sems.at[2]),
        pltpu.make_async_copy(wu_ref, gu.at[:, pl.ds(2 * units, units)], local_sems.at[3]),
        pltpu.make_async_copy(wd_ref, wd.at[pl.ds(0, units)], local_sems.at[4]),
    ]
    for copy in own:
        copy.start()

    def remote(src, dst, send, recv, device):
        return pltpu.make_async_remote_copy(
            src_ref=src, dst_ref=dst, send_sem=send, recv_sem=recv,
            device_id=device, device_id_type=MESH,
        )

    routes = routes_ref[...]
    codes = codes_ref[...].astype(F32)
    ratio = 2.5 * codes / jnp.sum(codes, axis=0, keepdims=True)
    named = [routes == f for f in range(FLIGHT)]
    matched = [jnp.sum(jnp.where(hit, 1.0, 0.0), axis=0, keepdims=True) for hit in named]
    weight = [jnp.sum(jnp.where(hit, ratio, 0.0), axis=0, keepdims=True) for hit in named]
    eight = (2 * FLIGHT, tokens)
    stacked = jnp.zeros(eight, F32)
    for f in range(FLIGHT):
        stacked = jnp.where(iota(eight, 0) == f, matched[f], stacked)
    upto = (iota((tokens, tokens), 0) <= iota((tokens, tokens), 1)).astype(F32).astype(BF16)
    rank = dot(stacked.astype(BF16), upto)
    slot = ((iota((UNIT, tokens), 0) & (CAP - 1)) + 1).astype(F32)
    for f in range(FLIGHT):
        here = jnp.where((matched[f] == 1.0) & (rank[f : f + 1] == slot), 1.0, 0.0)
        sel[pl.ds(UNIT * f, UNIT)] = here
        wsel[pl.ds(UNIT * f, UNIT)] = here * weight[f]

    def choose(block, out, scale):
        quarter_of = (iota((STACK, tokens), 0) // CAP) & (QUARTERS - 1)
        picks = [jnp.where(quarter_of == q, sel[...], 0.0).astype(BF16) for q in range(QUARTERS)]
        for i in range(quarter // COLS):
            total = sum(
                dot(picks[q], block[:, q * quarter + i * COLS : q * quarter + (i + 1) * COLS])
                for q in range(QUARTERS)
            )
            if scale is not None:
                total = total * scale
            out[:, :, i * COLS : (i + 1) * COLS] = total.astype(BF16).reshape(FLIGHT, UNIT, COLS)

    def x_copy(i, src, buf, k):
        return remote(
            src.at[plane[k]], buf.at[0, FLIGHT - k], x_send.at[i, k], x_recv.at[i, k], across[k]
        )

    def part_of(buf, place, first, n):
        return buf.at[place, pl.ds(first, n)]

    def gather_copy(kind, buf, order, way, i):
        hops, first, n = order[way][i]
        return remote(
            part_of(buf, FROM[way][hops], first, n), part_of(buf, FROM[way][hops + 1], first, n),
            ring_send.at[kind, way, i], ring_recv.at[kind, way, i], next_on[way],
        )

    arrived = set()

    def arrive(kind, src, buf, order, way, hops, first, n):
        if hops == 0:
            for j in range(max(first, 1), first + n):
                if (kind, j) not in arrived:
                    arrived.add((kind, j))
                    x_copy(kind, src, buf, FLIGHT - j).wait_recv()
            return
        for i, (h, f, m) in enumerate(order[way]):
            if h == hops - 1 and f < first + n and first < f + m and (kind, way, i) not in arrived:
                arrived.add((kind, way, i))
                gather_copy(kind, buf, order, way, i).wait_recv()

    def gather_step(kind, src, buf, order, i):
        for way in WAYS:
            arrive(kind, src, buf, order, way, *order[way][i])
            gather_copy(kind, buf, order, way, i).start()

    def gather_end(kind, src, buf, order):
        for hops in (3, 4):
            for way in WAYS:
                arrive(kind, src, buf, order, way, hops, 0, FLIGHT)

    def sum_copy(kind, part, recv, way, i):
        hops, first = SUMS[way][i]
        return remote(
            part_of(part, FROM[1 - way][hops], first, 2), recv.at[way, i],
            ring_send.at[kind, way, i], ring_recv.at[kind, way, i], next_on[way],
        )

    def sum_step(kind, part, recv, i):
        for way in WAYS:
            hops, first = SUMS[way][i]
            if i >= 2:
                sum_copy(kind, part, recv, way, i - 2).wait_recv()
                at_place = (FROM[1 - way][hops], pl.ds(first, 2))
                part[at_place] = (part[at_place].astype(F32) + recv[way, i - 2].astype(F32)).astype(BF16)
            sum_copy(kind, part, recv, way, i).start()

    def finish(kind, part, recv, got, targets, n):
        copies = []
        for i in (STEPS - 2, STEPS - 1):
            for way in WAYS:
                sum_copy(kind, part, recv, way, i).wait_recv()
        for first in (2, 0):
            came = {way: [i for i in (STEPS - 2, STEPS - 1) if SUMS[way][i][1] == first][0] for way in WAYS}
            at_place = (0, pl.ds(first, 2))
            total = part[at_place].astype(F32) + recv[LEFT, came[LEFT]].astype(F32)
            part[at_place] = (total + recv[RIGHT, came[RIGHT]].astype(F32)).astype(BF16)
            for j in (first, first + 1):
                copy = remote(part.at[0, j], got.at[x], fin_send.at[n, j], fin_recv.at[n, j], targets[j])
                copy.start()
                copies.append(copy)
        return copies

    def regrouping(dim):
        size = (STACK * QUARTERS, STACK * QUARTERS)
        n, m = iota(size, dim), iota(size, 1 - dim)
        low = n & (STACK - 1)
        there = (low // CAP) * UNIT + (n // STACK) * CAP + (low & (CAP - 1))
        return (m == there).astype(F32).astype(BF16)

    def cols_of(i, q=0):
        return pl.ds(pl.multiple_of(q * quarter + i * COLS, COLS), COLS)

    def natural(buf, group):
        def body(i, carry):
            block = buf[pl.ds(4 * group, 4), :, :, cols_of(i)].reshape(STACK * QUARTERS, COLS)
            got = dot(swap[...], block).astype(BF16)
            for q in range(QUARTERS):
                nat[pl.ds(STACK * group, STACK), cols_of(i, q)] = got[q * STACK : (q + 1) * STACK]
            return carry
        lax.fori_loop(0, quarter // COLS, body, 0)

    def blocked(product, part, first, last):
        def body(i, carry):
            pieces = [product(cols_of(i, q)).astype(BF16) for q in range(QUARTERS)]
            for group in range(count // STACK):
                block = jnp.concatenate([p[STACK * group : STACK * (group + 1)] for p in pieces], axis=0)
                got = tn(swap[...], block).astype(BF16)
                part[pl.ds(4 * group, 4), :, :, cols_of(i)] = got.reshape(4, FLIGHT, UNIT, COLS)
            return carry
        lax.fori_loop(first, last, body, 0)

    def gate_up(first, last):
        def body(i, carry):
            ks = pl.ds(pl.multiple_of(i * TILE, TILE), TILE)
            acc[...] += dot(nat[:, ks], gu[ks, :])
            return carry
        lax.fori_loop(first, last, body, 0)

    def activate():
        gate, upper = acc[:, : 2 * units], acc[:, 2 * units :]
        sigma = jax.nn.sigmoid(gate)
        silu = gate * sigma
        hid[...] = (silu * upper).astype(BF16)
        a_gate[...] = upper * sigma * (1.0 + gate * (1.0 - sigma))
        a_up[...] = silu

    def outputs(first, last):
        blocked(lambda cols: dot(hid[...], wd[:, cols]), part_y, first, last)

    def d_hidden(first, last):
        def body(i, carry):
            ks = pl.ds(pl.multiple_of(i * TILE, TILE), TILE)
            dh[...] += nt(nat[:, ks], wd[:, ks])
            return carry
        lax.fori_loop(first, last, body, 0)

    def d_activate():
        dgu[:, : 2 * units] = (dh[...] * a_gate[...]).astype(BF16)
        dgu[:, 2 * units :] = (dh[...] * a_up[...]).astype(BF16)

    def d_inputs(first, last):
        blocked(lambda cols: nt(dgu[...], gu[cols, :]), part_g, first, last)

    def place(weights, got, out):
        terms = weights.shape[1] // STACK
        quarter_of = (iota(weights.shape, 1) // CAP) & (QUARTERS - 1)
        left = jnp.concatenate(
            [jnp.where(quarter_of == q, weights, 0.0).astype(BF16) for q in range(QUARTERS)], axis=0
        )
        def body(i, carry):
            block = got[:, :, cols_of(i)].reshape(STACK, COLS)
            total = dot(left, jnp.concatenate([block] * terms, axis=0)).astype(BF16)
            for q in range(QUARTERS):
                out[:, cols_of(i, q)] = total[q * tokens : (q + 1) * tokens]
            return carry
        lax.fori_loop(0, quarter // COLS, body, 0)

    def three_terms(weights):
        high = weights.astype(BF16).astype(F32)
        mid = (weights - high).astype(BF16).astype(F32)
        low = (weights - high - mid).astype(BF16).astype(F32)
        ends = jnp.concatenate([low, jnp.zeros_like(low)], axis=0).T
        return jnp.concatenate([jnp.concatenate([high, mid], axis=0).T, ends[:, :STACK]], axis=1)

    tiles = width // TILE
    steps = quarter // COLS

    own[0].wait()
    choose(tok, pick_x, None)
    pl.semaphore_wait(barrier, len(peers))
    x_copies = [x_copy(0, pick_x, rows, k) for k in (1, 3, 2)]
    for copy in x_copies:
        copy.start()
    rows[0, 0] = pick_x[x]
    gather_step(0, pick_x, rows, ROWS, 0)
    small = [
        remote(wsel, wsel_in, s_send.at[0], s_recv.at[0], up[0]),
        remote(sel, sel_in, s_send.at[1], s_recv.at[1], down[0]),
    ]
    other = [
        remote(wg_ref, gu.at[:, pl.ds(units, units)], w_send.at[0], w_recv.at[0], sibling),
        remote(wu_ref, gu.at[:, pl.ds(3 * units, units)], w_send.at[1], w_recv.at[1], sibling),
        remote(wd_ref, wd.at[pl.ds(units, units)], w_send.at[2], w_recv.at[2], sibling),
    ]
    for copy in other + small:
        copy.start()
    for i in range(1, 4):
        gather_step(0, pick_x, rows, ROWS, i)
    own[1].wait()
    choose(cot, pick_g, jnp.sum(wsel[...], axis=1, keepdims=True))
    g_copies = [x_copy(1, pick_g, grads, k) for k in (1, 3, 2)]
    for copy in g_copies:
        copy.start()
    grads[0, 0] = pick_g[x]
    gather_step(0, pick_x, rows, ROWS, 4)
    swap[...] = regrouping(0)
    gather_step(0, pick_x, rows, ROWS, 5)
    acc[...] = jnp.zeros_like(acc)
    dh[...] = jnp.zeros_like(dh)
    for i in range(6, len(ROWS[LEFT])):
        gather_step(0, pick_x, rows, ROWS, i)

    gather_step(1, pick_g, grads, GRADS, 0)
    gather_step(1, pick_g, grads, GRADS, 1)
    gather_end(0, pick_x, rows, ROWS)
    natural(rows, 0)
    natural(rows, 1)
    for copy in own[2:]:
        copy.wait()
    for copy in other:
        copy.wait_recv()
    gather_step(1, pick_g, grads, GRADS, 2)
    gate_up(0, tiles // 2)
    gather_step(1, pick_g, grads, GRADS, 3)
    gate_up(tiles // 2, tiles)
    activate()
    gather_step(1, pick_g, grads, GRADS, 4)
    outputs(0, steps // 2)
    gather_step(1, pick_g, grads, GRADS, 5)
    outputs(steps // 2, steps)
    gather_step(1, pick_g, grads, GRADS, 6)

    sum_step(2, part_y, recv_y, 0)
    sum_step(2, part_y, recv_y, 1)
    gather_end(1, pick_g, grads, GRADS)
    natural(grads, 0)
    natural(grads, 1)
    sum_step(2, part_y, recv_y, 2)
    d_hidden(0, tiles)
    d_activate()
    sum_step(2, part_y, recv_y, 3)
    d_inputs(0, steps // 2)
    sum_step(2, part_y, recv_y, 4)
    d_inputs(steps // 2, steps)
    sum_step(2, part_y, recv_y, 5)
    sum_step(2, part_y, recv_y, 6)

    sum_step(3, part_g, recv_g, 0)
    sum_step(3, part_g, recv_g, 1)
    done_y = finish(2, part_y, recv_y, got_y, up, 0)
    sum_step(3, part_g, recv_g, 2)
    small[0].wait_recv()
    weights_y = three_terms(wsel_in[...])
    small[1].wait_recv()
    weights_g = jnp.concatenate([sel_in[...], jnp.zeros_like(sel_in)], axis=0).T[:, :STACK]
    sum_step(3, part_g, recv_g, 3)
    for copy in done_y:
        copy.wait_recv()
    place(weights_y, got_y, out_ref)
    for i in range(4, STEPS):
        sum_step(3, part_g, recv_g, i)
    done_g = finish(3, part_g, recv_g, got_g, down, 1)

    for copy in x_copies + g_copies + other + small + done_y:
        copy.wait_send()
    for way in WAYS:
        for i in range(len(ROWS[way])):
            gather_copy(0, rows, ROWS, way, i).wait_send()
        for i in range(STEPS):
            gather_copy(1, grads, GRADS, way, i).wait_send()
            sum_copy(2, part_y, recv_y, way, i).wait_send()
            sum_copy(3, part_g, recv_g, way, i).wait_send()
    for copy in done_g:
        copy.wait_recv()
    place(weights_g, got_g, grad_ref)
    for copy in done_g:
        copy.wait_send()


def on_device(section_input, cotangent, routes, gate_codes, w_gate, w_up, w_down):
    tokens, width = section_input.shape[1:]
    quarter = width // QUARTERS
    units = w_gate.shape[2]
    count = RING * FLIGHT * CAP
    vmem = pl.BlockSpec(memory_space=pltpu.VMEM)
    hbm = pl.BlockSpec(memory_space=pltpu.HBM)
    dma = pltpu.SemaphoreType.DMA
    blocks = pltpu.VMEM((FLIGHT, UNIT, quarter), BF16)
    gathered = pltpu.VMEM((RING, FLIGHT, UNIT, quarter), BF16)
    incoming = pltpu.VMEM((2, STEPS, 2, UNIT, quarter), BF16)
    block = pltpu.VMEM((tokens, width), BF16)
    half_wide = pltpu.VMEM((count, 2 * units), F32)
    select = pltpu.VMEM((STACK, tokens), F32)
    most = len(ROWS[LEFT])
    passed, grad_passed = pl.pallas_call(
        exchange,
        out_shape=(jax.ShapeDtypeStruct((tokens, width), BF16),) * 2,
        in_specs=[vmem] * 2 + [hbm] * 5,
        out_specs=(vmem,) * 2,
        scratch_shapes=[
            block, block, blocks, blocks, gathered, gathered,
            pltpu.VMEM((count, width), BF16),
            pltpu.VMEM((width, 4 * units), BF16),
            pltpu.VMEM((2 * units, width), BF16),
            pltpu.VMEM((STACK * QUARTERS, STACK * QUARTERS), BF16),
            pltpu.VMEM((count, 4 * units), F32),
            half_wide,
            half_wide,
            pltpu.VMEM((count, 2 * units), BF16),
            half_wide,
            pltpu.VMEM((count, 4 * units), BF16),
            gathered, gathered, incoming, incoming, blocks, blocks,
            select, select, select, select,
            dma((5,)),
            dma((3,)), dma((3,)),
            dma((2, FLIGHT)), dma((2, FLIGHT)),
            dma((2,)), dma((2,)),
            dma((4, 2, most)), dma((4, 2, most)),
            dma((2, FLIGHT)), dma((2, FLIGHT)),
        ],
        compiler_params=pltpu.CompilerParams(
            collective_id=0, has_side_effects=True, vmem_limit_bytes=59 * 2**20
        ),
        cost_estimate=pl.CostEstimate(
            flops=24 * count * width * units, bytes_accessed=14 * tokens * width, transcendentals=0
        ),
        name="exchange",
    )(routes[0].T, gate_codes[0].T, section_input[0], cotangent[0], w_gate[0], w_up[0], w_down[0])
    return passed[None], grad_passed[None]


def solution(mesh):
    placed = (
        P("pipe", "expert", None),
        P("pipe", "expert", None),
        P("pipe", "expert", None),
        P("pipe", "expert", None),
        P("pipe", None, "expert"),
        P("pipe", None, "expert"),
        P("pipe", "expert", None),
    )
    return jax.shard_map(
        on_device,
        mesh=mesh,
        in_specs=placed,
        out_specs=(P("pipe", "expert", None), P("pipe", "expert", None)),
        check_vma=False,
    )
```

time: 455 us -> 101 us (0.22)
  waiting for transfers between devices: 349 us -> 0 us
  Pallas kernels: 0 us -> 95.6 us
  local copies, waits for them, and re-layouts: 38.5 us -> 4.21 us
  starting transfers between devices: 31.8 us -> 0 us
  matrix products: 23.9 us -> 0 us
  other arithmetic: 8.52 us -> 0 us
    all_to_all x4 -> x0, waiting for transfers between devices: 307 us -> none  [the longest x1 82.5 us: on_device(): lax.all_to_all(spread_rows, 'expert', split_axis=0, concat_axis=0, tiled=...]
    pallas_call x0 -> x1, Pallas kernels: none -> 95.6 us  [on_device(): pl.pallas_call(exchange, out_shape=(jax.ShapeDtypeStruct((tokens, width),...]
    ppermute x2 -> x0, waiting for transfers between devices: 41.8 us -> none  [from_behind(): return lax.ppermute(block, axis, route)]
    all_to_all x4 -> x0, starting transfers between devices: 30.7 us -> none  [the longest x1 12.3 us: on_device(): lax.all_to_all(spread_rows, 'expert', split_axis=0, concat_axis=0, tiled=...]
    reshape x4 -> x0, local copies, waits for them, and re-layouts: 27.5 us -> none  [the longest x1 7.02 us: on_device(): grad_part.reshape(devices, CAP, width)]
    dot_general x11 -> x0, matrix products: 23.9 us -> none  [the longest x3 7.76 us: contract_rows(): lax.dot_general(left, right, (((1,), (1,)), ((), ())), preferred_element_...]
    reduce_sum x5 -> x0, other arithmetic: 8.17 us -> none  [the longest x1 3.65 us: on_device(): jnp.sum(grad_back.astype(jnp.float32).reshape(flight, group, CAP, width),...]
    broadcast_in_dim x2 -> x0, local copies, waits for them, and re-layouts: 5.91 us -> none  [the longest x1 3.01 us: on_device(): spread_grads = jnp.repeat(send_grads, group, axis=0)]
  transfers between devices with their start and end apart: 6 -> 0, of which waited for: 5 -> 0; matrix products, arithmetic and copies ran while one was open for 8% -> 0% of each run, Pallas kernels for 0% -> 0%
where the time goes in v3:
time: 101 us
  Pallas kernels  95.6 us (95%)
  local copies, waits for them, and re-layouts  4.21 us (4%)
    pallas_call x1, Pallas kernels, on_device(): pl.pallas_call(exchange, out_shape=(jax.ShapeDtypeStruct((tokens, width),...  95.6 us
    unnamed x4, local copies, waits for them, and re-layouts  4.21 us

profile of v3, /device:TPU:24, one launch (start us, length us, event | category | flops | bytes accessed | tf_op | source)
XLA Modules:
  0.0 100.5 jit_solution(15821932989302028075)
XLA Ops:
  0.6 95.6 %exchange.1 = (bf16[128,7168]{1,0:T(8,128)(2,1)}, bf16[128,7168]{1,0:T(8,128)(2,1)}) custom-call(s32[8,128]{1,0:T(8,128)} %bitcast.20, s32[8,128]{1,0:T(8,128)} %bitcast.21, bf16[128,7168]{1,0:T(8,128)(2,1)} %bitcast.15, bf16[128,7168]{1,0:T(8,128)(2,1)} %bitcast.16, bf16[7168,128]{1,0:T(8,128)(2,1)} %bitcast.17, bf16[7168,128]{1,0:T(8,128)(2,1)} %bitcast.18, ...), custom_call_target="tpu_custom_call" | custom-call | flops 2818572288 | bytes 12845056 | tf_op jit(solution)/shard_map/exchange/pallas_call | solution.py:413
  96.3 0.0 copy-start
  96.3 3.0 %copy.11 = bf16[1,128,7168]{2,1,0:T(8,128)(2,1)} copy(bf16[1,128,7168]{2,1,0:T(8,128)(2,1)} %bitcast.14) | data formatting | bytes 3670016
  99.3 0.0 copy-done
  99.3 1.2 %copy.12 = bf16[1,128,7168]{2,1,0:T(8,128)(2,1)} copy(bf16[1,128,7168]{2,1,0:T(8,128)(2,1)S(1)} %bitcast.13) | data formatting | bytes 3670016
Async XLA Ops:
  96.3 3.0 %copy-start = (bf16[128,7168]{1,0:T(8,128)(2,1)S(1)}, bf16[128,7168]{1,0:T(8,128)(2,1)}, u32[]{:S(2)}) copy-start(bf16[128,7168]{1,0:T(8,128)(2,1)} %get-tuple-element.5) | copy-start | bytes 5505028

commit v4 on v3

--- a/solution.py
+++ b/solution.py
@@ -22,18 +22,19 @@
 WAYS = (RIGHT, LEFT)
 FROM = {RIGHT: (0, 1, 3, 5, 7), LEFT: (0, 2, 4, 6, 7)}
 ROWS = {
-    RIGHT: ((0, 0, 1), (0, 1, 1), (0, 2, 1), (0, 3, 1), (1, 0, 2), (1, 2, 2), (2, 0, 2), (2, 2, 2), (3, 0, 2)),
-    LEFT: ((0, 0, 1), (0, 3, 1), (0, 2, 1), (0, 1, 1), (1, 2, 2), (1, 0, 2), (2, 2, 2), (2, 0, 2), (3, 2, 2)),
+    RIGHT: tuple((hops, j, 1) for hops, order in ((0, (0, 1, 3, 2)), (1, (0, 1, 3, 2)), (2, (0, 1, 3, 2)), (3, (0, 1))) for j in order),
+    LEFT: tuple((hops, j, 1) for hops, order in ((0, (0, 3, 1, 2)), (1, (3, 0, 2, 1)), (2, (3, 2, 0, 1)), (3, (3, 2))) for j in order),
 }
-GRADS = {
-    RIGHT: ((0, 0, 2), (0, 2, 2), (1, 0, 2), (1, 2, 2), (2, 0, 2), (2, 2, 2), (3, 0, 2)),
-    LEFT: ((0, 2, 2), (0, 0, 2), (1, 2, 2), (1, 0, 2), (2, 2, 2), (2, 0, 2), (3, 2, 2)),
+GRADS = ROWS
+LAST = (1, 2, 3, 0)
+ENDS = {
+    LEFT: tuple((hops, j, 1) for hops, order in ((4, (1, 3)), (3, (2, 0, 1, 3)), (2, (2, 1, 0, 3)), (1, LAST)) for j in order),
+    RIGHT: tuple((hops, j, 1) for hops, order in ((4, (2, 0)), (3, (1, 3, 2, 0)), (2, (1, 3, 2, 0)), (1, LAST)) for j in order),
 }
-SUMS = {
-    LEFT: ((4, 0), (3, 2), (3, 0), (2, 2), (2, 0), (1, 2), (1, 0)),
-    RIGHT: ((4, 2), (3, 0), (3, 2), (2, 0), (2, 2), (1, 0), (1, 2)),
-}
-STEPS = len(SUMS[LEFT])
+OUTS = ENDS
+STEPS = len(ENDS[LEFT])
+ORDERS = (ROWS, GRADS, OUTS, ENDS)
+MOST = max(len(order[way]) for order in ORDERS for way in WAYS)
 
 
 def nt(left, right):
@@ -53,10 +54,10 @@
 
 
 def exchange(
-    routes_ref, codes_ref, tok_hbm, cot_hbm, wg_ref, wu_ref, wd_ref,
-    out_ref, grad_ref,
-    tok, cot, pick_x, pick_g, rows, grads, nat, gu, wd, swap, acc, a_gate, a_up, hid, dh, dgu,
-    part_y, part_g, recv_y, recv_g, got_y, got_g, sel, wsel, sel_in, wsel_in,
+    routes_hbm, codes_hbm, tok_hbm, cot_hbm, wg_ref, wu_ref, wd_ref,
+    out_hbm, got_g, left_hbm,
+    out_ref, left_ref, routes_ref, codes_ref, tok, cot, pick_x, pick_g, rows, grads, nat, gu, wd, swap, acc, a_gate, a_up, hid, dh, dgu,
+    part_y, part_g, recv_y, recv_g, got_y, sel, wsel, sel_in, wsel_in,
     local_sems, w_send, w_recv, x_send, x_recv, s_send, s_recv,
     ring_send, ring_recv, fin_send, fin_recv,
 ):
@@ -86,20 +87,22 @@
     up = [at(xx, z, core, ahead) for xx in plane]
     down = [at(xx, z, core, behind) for xx in plane]
 
-    barrier = pltpu.get_barrier_semaphore()
-    peers = [sibling, next_on[RIGHT], next_on[LEFT]] + across[1:] + up + down
-    for peer in peers:
-        pl.semaphore_signal(barrier, inc=1, device_id=peer, device_id_type=MESH)
-
     own = [
+        pltpu.make_async_copy(routes_hbm, routes_ref, local_sems.at[5]),
+        pltpu.make_async_copy(codes_hbm, codes_ref, local_sems.at[6]),
         pltpu.make_async_copy(tok_hbm, tok, local_sems.at[0]),
         pltpu.make_async_copy(cot_hbm, cot, local_sems.at[1]),
         pltpu.make_async_copy(wg_ref, gu.at[:, pl.ds(0, units)], local_sems.at[2]),
         pltpu.make_async_copy(wu_ref, gu.at[:, pl.ds(2 * units, units)], local_sems.at[3]),
         pltpu.make_async_copy(wd_ref, wd.at[pl.ds(0, units)], local_sems.at[4]),
     ]
-    for copy in own:
-        copy.start()
+    for copy in own[:3]:
+        copy.start()
+
+    barrier = pltpu.get_barrier_semaphore()
+    peers = [sibling, next_on[RIGHT], next_on[LEFT]] + across[1:] + up + down
+    for peer in peers:
+        pl.semaphore_signal(barrier, inc=1, device_id=peer, device_id_type=MESH)
 
     def remote(src, dst, send, recv, device):
         return pltpu.make_async_remote_copy(
@@ -107,6 +110,8 @@
             device_id=device, device_id_type=MESH,
         )
 
+    own[0].wait()
+    own[1].wait()
     routes = routes_ref[...]
     codes = codes_ref[...].astype(F32)
     ratio = 2.5 * codes / jnp.sum(codes, axis=0, keepdims=True)
@@ -125,10 +130,10 @@
         sel[pl.ds(UNIT * f, UNIT)] = here
         wsel[pl.ds(UNIT * f, UNIT)] = here * weight[f]
 
-    def choose(block, out, scale):
+    def choose(block, out, scale, first, last):
         quarter_of = (iota((STACK, tokens), 0) // CAP) & (QUARTERS - 1)
         picks = [jnp.where(quarter_of == q, sel[...], 0.0).astype(BF16) for q in range(QUARTERS)]
-        for i in range(quarter // COLS):
+        for i in range(first, last):
             total = sum(
                 dot(picks[q], block[:, q * quarter + i * COLS : q * quarter + (i + 1) * COLS])
                 for q in range(QUARTERS)
@@ -177,35 +182,42 @@
                 arrive(kind, src, buf, order, way, hops, 0, FLIGHT)
 
     def sum_copy(kind, part, recv, way, i):
-        hops, first = SUMS[way][i]
+        hops, first, n = ORDERS[kind][way][i]
         return remote(
-            part_of(part, FROM[1 - way][hops], first, 2), recv.at[way, i],
+            part_of(part, FROM[1 - way][hops], first, n), recv.at[way, hops - 1, pl.ds(first, n)],
             ring_send.at[kind, way, i], ring_recv.at[kind, way, i], next_on[way],
         )
 
+    def sum_arrive(kind, part, recv, way, hops, first, n):
+        came = False
+        for i, (h, f, m) in enumerate(ORDERS[kind][way]):
+            if h == hops + 1 and f < first + n and first < f + m:
+                came = True
+                if (kind, way, i) not in arrived:
+                    arrived.add((kind, way, i))
+                    sum_copy(kind, part, recv, way, i).wait_recv()
+        return came
+
     def sum_step(kind, part, recv, i):
         for way in WAYS:
-            hops, first = SUMS[way][i]
-            if i >= 2:
-                sum_copy(kind, part, recv, way, i - 2).wait_recv()
-                at_place = (FROM[1 - way][hops], pl.ds(first, 2))
-                part[at_place] = (part[at_place].astype(F32) + recv[way, i - 2].astype(F32)).astype(BF16)
+            hops, first, n = ORDERS[kind][way][i]
+            if sum_arrive(kind, part, recv, way, hops, first, n):
+                here, there = (FROM[1 - way][hops], pl.ds(first, n)), (way, hops, pl.ds(first, n))
+                part[here] = (part[here].astype(F32) + recv[there].astype(F32)).astype(BF16)
             sum_copy(kind, part, recv, way, i).start()
 
-    def finish(kind, part, recv, got, targets, n):
+    def finish(kind, part, recv, got, targets, order):
         copies = []
-        for i in (STEPS - 2, STEPS - 1):
+        for j in order:
             for way in WAYS:
-                sum_copy(kind, part, recv, way, i).wait_recv()
-        for first in (2, 0):
-            came = {way: [i for i in (STEPS - 2, STEPS - 1) if SUMS[way][i][1] == first][0] for way in WAYS}
-            at_place = (0, pl.ds(first, 2))
-            total = part[at_place].astype(F32) + recv[LEFT, came[LEFT]].astype(F32)
-            part[at_place] = (total + recv[RIGHT, came[RIGHT]].astype(F32)).astype(BF16)
-            for j in (first, first + 1):
-                copy = remote(part.at[0, j], got.at[x], fin_send.at[n, j], fin_recv.at[n, j], targets[j])
-                copy.start()
-                copies.append(copy)
+                sum_arrive(kind, part, recv, way, 0, j, 1)
+            total = part[0, j].astype(F32) + recv[LEFT, 0, j].astype(F32)
+            part[0, j] = (total + recv[RIGHT, 0, j].astype(F32)).astype(BF16)
+            copy = remote(
+                part.at[0, j], got.at[x], fin_send.at[kind - 2, j], fin_recv.at[kind - 2, j], targets[j]
+            )
+            copy.start()
+            copies.append(copy)
         return copies
 
     def regrouping(dim):
@@ -269,12 +281,14 @@
     def d_inputs(first, last):
         blocked(lambda cols: nt(dgu[...], gu[cols, :]), part_g, first, last)
 
-    def place(weights, got, out):
-        terms = weights.shape[1] // STACK
+    def by_quarter(weights):
         quarter_of = (iota(weights.shape, 1) // CAP) & (QUARTERS - 1)
-        left = jnp.concatenate(
+        return jnp.concatenate(
             [jnp.where(quarter_of == q, weights, 0.0).astype(BF16) for q in range(QUARTERS)], axis=0
         )
+
+    def place(left, got, out):
+        terms = left.shape[1] // STACK
         def body(i, carry):
             block = got[:, :, cols_of(i)].reshape(STACK, COLS)
             total = dot(left, jnp.concatenate([block] * terms, axis=0)).astype(BF16)
@@ -293,14 +307,43 @@
     tiles = width // TILE
     steps = quarter // COLS
 
-    own[0].wait()
-    choose(tok, pick_x, None)
+    own[2].wait()
+    own[3].start()
+    choose(tok, pick_x, None, 0, steps)
     pl.semaphore_wait(barrier, len(peers))
     x_copies = [x_copy(0, pick_x, rows, k) for k in (1, 3, 2)]
     for copy in x_copies:
         copy.start()
     rows[0, 0] = pick_x[x]
-    gather_step(0, pick_x, rows, ROWS, 0)
+    def row_steps(*which):
+        for i in which:
+            gather_step(0, pick_x, rows, ROWS, i)
+
+    def grad_steps(*which):
+        for i in which:
+            gather_step(1, pick_g, grads, GRADS, i)
+
+    def out_steps(*which):
+        for i in which:
+            sum_step(2, part_y, recv_y, i)
+
+    def end_steps(*which):
+        for i in which:
+            sum_step(3, part_g, recv_g, i)
+
+    row_steps(0)
+    own[3].wait()
+    for copy in own[4:]:
+        copy.start()
+    choose(cot, pick_g, jnp.sum(wsel[...], axis=1, keepdims=True), 0, steps)
+    g_copies = [x_copy(1, pick_g, grads, k) for k in (1, 3, 2)]
+    for copy in g_copies:
+        copy.start()
+    grads[0, 0] = pick_g[x]
+    grad_steps(0)
+    row_steps(1, 2)
+    grad_steps(1, 2)
+    row_steps(3, 4)
     small = [
         remote(wsel, wsel_in, s_send.at[0], s_recv.at[0], up[0]),
         remote(sel, sel_in, s_send.at[1], s_recv.at[1], down[0]),
@@ -312,87 +355,132 @@
     ]
     for copy in other + small:
         copy.start()
-    for i in range(1, 4):
-        gather_step(0, pick_x, rows, ROWS, i)
-    own[1].wait()
-    choose(cot, pick_g, jnp.sum(wsel[...], axis=1, keepdims=True))
-    g_copies = [x_copy(1, pick_g, grads, k) for k in (1, 3, 2)]
-    for copy in g_copies:
-        copy.start()
-    grads[0, 0] = pick_g[x]
-    gather_step(0, pick_x, rows, ROWS, 4)
+    row_steps(5, 6)
     swap[...] = regrouping(0)
-    gather_step(0, pick_x, rows, ROWS, 5)
+    row_steps(7, 8)
     acc[...] = jnp.zeros_like(acc)
     dh[...] = jnp.zeros_like(dh)
-    for i in range(6, len(ROWS[LEFT])):
-        gather_step(0, pick_x, rows, ROWS, i)
-
-    gather_step(1, pick_g, grads, GRADS, 0)
-    gather_step(1, pick_g, grads, GRADS, 1)
+    row_steps(9, 10, 11, 12, 13)
+    grad_steps(3, 4)
+    arrive(0, pick_x, rows, ROWS, RIGHT, 2, 0, FLIGHT)
+    natural(rows, 0)
+    grad_steps(5)
+
     gather_end(0, pick_x, rows, ROWS)
-    natural(rows, 0)
     natural(rows, 1)
-    for copy in own[2:]:
+    for copy in own[4:]:
         copy.wait()
     for copy in other:
         copy.wait_recv()
-    gather_step(1, pick_g, grads, GRADS, 2)
+    grad_steps(6)
     gate_up(0, tiles // 2)
-    gather_step(1, pick_g, grads, GRADS, 3)
+    grad_steps(7, 8)
     gate_up(tiles // 2, tiles)
     activate()
-    gather_step(1, pick_g, grads, GRADS, 4)
-    outputs(0, steps // 2)
-    gather_step(1, pick_g, grads, GRADS, 5)
-    outputs(steps // 2, steps)
-    gather_step(1, pick_g, grads, GRADS, 6)
-
-    sum_step(2, part_y, recv_y, 0)
-    sum_step(2, part_y, recv_y, 1)
+    grad_steps(9, 10)
+    outputs(0, 2)
+    grad_steps(11)
+    outputs(2, 4)
+    grad_steps(12)
+    outputs(4, 6)
+    grad_steps(13)
+    outputs(6, steps)
+
+    out_steps(0, 1)
+    arrive(1, pick_g, grads, GRADS, RIGHT, 2, 0, FLIGHT)
+    natural(grads, 0)
+    out_steps(2)
     gather_end(1, pick_g, grads, GRADS)
-    natural(grads, 0)
     natural(grads, 1)
-    sum_step(2, part_y, recv_y, 2)
+    out_steps(3)
     d_hidden(0, tiles)
     d_activate()
-    sum_step(2, part_y, recv_y, 3)
-    d_inputs(0, steps // 2)
-    sum_step(2, part_y, recv_y, 4)
-    d_inputs(steps // 2, steps)
-    sum_step(2, part_y, recv_y, 5)
-    sum_step(2, part_y, recv_y, 6)
-
-    sum_step(3, part_g, recv_g, 0)
-    sum_step(3, part_g, recv_g, 1)
-    done_y = finish(2, part_y, recv_y, got_y, up, 0)
-    sum_step(3, part_g, recv_g, 2)
+    out_steps(4, 5)
+    d_inputs(0, 2)
+    out_steps(6, 7)
+    d_inputs(2, 4)
+    out_steps(8, 9)
+    d_inputs(4, 6)
+    out_steps(10, 11)
+    d_inputs(6, steps)
+    out_steps(12)
+    end_steps(0, 1)
+    out_steps(13)
+    end_steps(2, 3)
+
+    done_y = finish(2, part_y, recv_y, got_y, up, LAST)
+    end_steps(4, 5)
     small[0].wait_recv()
-    weights_y = three_terms(wsel_in[...])
+    weights_y = by_quarter(three_terms(wsel_in[...]))
     small[1].wait_recv()
-    weights_g = jnp.concatenate([sel_in[...], jnp.zeros_like(sel_in)], axis=0).T[:, :STACK]
-    sum_step(3, part_g, recv_g, 3)
+    left_ref[...] = by_quarter(jnp.concatenate([sel_in[...], jnp.zeros_like(sel_in)], axis=0).T[:, :STACK])
+    end_steps(6, 7)
     for copy in done_y:
         copy.wait_recv()
     place(weights_y, got_y, out_ref)
-    for i in range(4, STEPS):
-        sum_step(3, part_g, recv_g, i)
-    done_g = finish(3, part_g, recv_g, got_g, down, 1)
-
+    results = [
+        pltpu.make_async_copy(out_ref, out_hbm, local_sems.at[7]),
+        pltpu.make_async_copy(left_ref, left_hbm, local_sems.at[8]),
+    ]
+    for copy in results:
+        copy.start()
+    end_steps(8, 9)
     for copy in x_copies + g_copies + other + small + done_y:
         copy.wait_send()
-    for way in WAYS:
-        for i in range(len(ROWS[way])):
+    end_steps(10, 11, 12, 13)
+    for i in range(STEPS):
+        for way in WAYS:
             gather_copy(0, rows, ROWS, way, i).wait_send()
-        for i in range(STEPS):
             gather_copy(1, grads, GRADS, way, i).wait_send()
             sum_copy(2, part_y, recv_y, way, i).wait_send()
+    done_g = finish(3, part_g, recv_g, got_g, down, LAST)
+    for i in range(STEPS):
+        for way in WAYS:
             sum_copy(3, part_g, recv_g, way, i).wait_send()
-    for copy in done_g:
-        copy.wait_recv()
-    place(weights_g, got_g, grad_ref)
-    for copy in done_g:
-        copy.wait_send()
+    for copy in done_g + results:
+        copy.wait()
+
+
+def write_out(y_hbm, g_hbm, left_hbm, out_hbm, grad_hbm, y_ref, g_ref, left_ref, dense, in_sems, y_sems, sems):
+    tokens, width = y_hbm.shape
+    quarter = width // QUARTERS
+    needed = [
+        pltpu.make_async_copy(g_hbm, g_ref, in_sems.at[0]),
+        pltpu.make_async_copy(left_hbm, left_ref, in_sems.at[1]),
+    ]
+    for copy in needed:
+        copy.start()
+    part = tokens // QUARTERS
+    here = []
+    for n in range(QUARTERS):
+        rows = pl.ds(n * part, part)
+        here.append(pltpu.make_async_copy(y_hbm.at[rows], y_ref.at[rows], in_sems.at[2 + n]))
+        here[n].start()
+    for copy in needed:
+        copy.wait()
+    left = left_ref[...]
+    copies = []
+    for n in range(QUARTERS):
+        rows = pl.ds(n * part, part)
+        here[n].wait()
+        copies.append(pltpu.make_async_copy(y_ref.at[rows], out_hbm.at[rows], y_sems.at[n]))
+        copies[n].start()
+    cuts = (0, 3, 5, 7)
+    for n in range(len(cuts) - 1):
+        for i in range(cuts[n], cuts[n + 1]):
+            block = g_ref[:, :, i * COLS : (i + 1) * COLS].reshape(STACK, COLS)
+            total = dot(left, block).astype(BF16)
+            for q in range(QUARTERS):
+                dense[:, q * quarter + i * COLS : q * quarter + (i + 1) * COLS] = total[q * tokens : (q + 1) * tokens]
+        for q in range(QUARTERS):
+            cols = pl.ds(q * quarter + cuts[n] * COLS, (cuts[n + 1] - cuts[n]) * COLS)
+            copy = pltpu.make_async_copy(
+                dense.at[:, cols], grad_hbm.at[:, cols], sems.at[n * QUARTERS + q]
+            )
+            copy.start()
+            copies.append(copy)
+    for copy in copies:
+        copy.wait()
 
 
 def on_device(section_input, cotangent, routes, gate_codes, w_gate, w_up, w_down):
@@ -400,23 +488,27 @@
     quarter = width // QUARTERS
     units = w_gate.shape[2]
     count = RING * FLIGHT * CAP
-    vmem = pl.BlockSpec(memory_space=pltpu.VMEM)
     hbm = pl.BlockSpec(memory_space=pltpu.HBM)
     dma = pltpu.SemaphoreType.DMA
     blocks = pltpu.VMEM((FLIGHT, UNIT, quarter), BF16)
     gathered = pltpu.VMEM((RING, FLIGHT, UNIT, quarter), BF16)
-    incoming = pltpu.VMEM((2, STEPS, 2, UNIT, quarter), BF16)
+    incoming = pltpu.VMEM((2, 4, FLIGHT, UNIT, quarter), BF16)
     block = pltpu.VMEM((tokens, width), BF16)
+    route = pltpu.VMEM(routes.shape[:0:-1], jnp.int32)
     half_wide = pltpu.VMEM((count, 2 * units), F32)
     select = pltpu.VMEM((STACK, tokens), F32)
-    most = len(ROWS[LEFT])
-    passed, grad_passed = pl.pallas_call(
+    dense = jax.ShapeDtypeStruct((tokens, width), BF16)
+    out_dense, got_g, left = pl.pallas_call(
         exchange,
-        out_shape=(jax.ShapeDtypeStruct((tokens, width), BF16),) * 2,
-        in_specs=[vmem] * 2 + [hbm] * 5,
-        out_specs=(vmem,) * 2,
+        out_shape=(
+            dense,
+            jax.ShapeDtypeStruct((FLIGHT, UNIT, quarter), BF16),
+            jax.ShapeDtypeStruct((QUARTERS * tokens, STACK), BF16),
+        ),
+        in_specs=[hbm] * 7,
+        out_specs=(hbm,) * 3,
         scratch_shapes=[
-            block, block, blocks, blocks, gathered, gathered,
+            block, pltpu.VMEM((QUARTERS * tokens, STACK), BF16), route, route, block, block, blocks, blocks, gathered, gathered,
             pltpu.VMEM((count, width), BF16),
             pltpu.VMEM((width, 4 * units), BF16),
             pltpu.VMEM((2 * units, width), BF16),
@@ -427,23 +519,35 @@
             pltpu.VMEM((count, 2 * units), BF16),
             half_wide,
             pltpu.VMEM((count, 4 * units), BF16),
-            gathered, gathered, incoming, incoming, blocks, blocks,
+            gathered, gathered, incoming, incoming, blocks,
             select, select, select, select,
-            dma((5,)),
+            dma((9,)),
             dma((3,)), dma((3,)),
             dma((2, FLIGHT)), dma((2, FLIGHT)),
             dma((2,)), dma((2,)),
-            dma((4, 2, most)), dma((4, 2, most)),
+            dma((4, 2, MOST)), dma((4, 2, MOST)),
             dma((2, FLIGHT)), dma((2, FLIGHT)),
         ],
         compiler_params=pltpu.CompilerParams(
-            collective_id=0, has_side_effects=True, vmem_limit_bytes=59 * 2**20
+            collective_id=0, has_side_effects=True, vmem_limit_bytes=57 * 2**20
         ),
         cost_estimate=pl.CostEstimate(
             flops=24 * count * width * units, bytes_accessed=14 * tokens * width, transcendentals=0
         ),
         name="exchange",
     )(routes[0].T, gate_codes[0].T, section_input[0], cotangent[0], w_gate[0], w_up[0], w_down[0])
+    passed, grad_passed = pl.pallas_call(
+        write_out,
+        out_shape=(dense,) * 2,
+        in_specs=[hbm] * 3,
+        out_specs=(hbm,) * 2,
+        scratch_shapes=[
+            block, blocks, pltpu.VMEM((QUARTERS * tokens, STACK), BF16), block,
+            dma((2 + QUARTERS,)), dma((QUARTERS,)), dma((3 * QUARTERS,)),
+        ],
+        compiler_params=pltpu.CompilerParams(vmem_limit_bytes=57 * 2**20),
+        name="write_out",
+    )(out_dense, got_g, left)
     return passed[None], grad_passed[None]
 
 

time: 101 us -> 95.4 us (0.945)
  local copies, waits for them, and re-layouts: 4.21 us -> 0 us
    unnamed x4 -> x0, local copies, waits for them, and re-layouts: 4.21 us -> none
    pallas_call x1 -> x2, Pallas kernels: 95.6 us -> 94.6 us  [the longest x1 91.3 us: on_device(): pl.pallas_call(exchange, out_shape=(dense, jax.ShapeDtypeStruct((FLIGHT,...]
where the time goes in v4:
time: 95.4 us; the launch traced here: 95.3 us
  Pallas kernels  94.6 us (99%)
    pallas_call x1, Pallas kernels, on_device(): pl.pallas_call(exchange, out_shape=(dense, jax.ShapeDtypeStruct((FLIGHT,...  91.3 us
    pallas_call x1, Pallas kernels, on_device(): pl.pallas_call(write_out, out_shape=(dense,) * 2, in_specs=[hbm] * 3, out...  3.36 us

profile of v4, /device:TPU:24, one launch (start us, length us, event | category | flops | bytes accessed | tf_op | source)
XLA Modules:
  0.0 95.3 jit_solution(18210601032853642233)
XLA Ops:
  0.6 91.3 %exchange.1 = (bf16[128,7168]{1,0:T(8,128)(2,1)}, bf16[4,16,1792]{2,1,0:T(8,128)(2,1)}, bf16[512,64]{1,0:T(8,128)(2,1)}) custom-call(s32[8,128]{1,0:T(8,128)} %bitcast.20, s32[8,128]{1,0:T(8,128)} %bitcast.21, bf16[128,7168]{1,0:T(8,128)(2,1)} %bitcast.13, bf16[128,7168]{1,0:T(8,128)(2,1)} %bitcast.14, bf16[7168,128]{1,0:T(8,128)(2,1)} %bitcast.15, ...), custom_call_target="tpu_custom_call" | custom-call | flops 2818572288 | bytes 12845056 | tf_op jit(solution)/shard_map/exchange/pallas_call | solution.py:501
  91.9 3.4 %write_out.1 = (bf16[128,7168]{1,0:T(8,128)(2,1)}, bf16[128,7168]{1,0:T(8,128)(2,1)}) custom-call(bf16[128,7168]{1,0:T(8,128)(2,1)} %get-tuple-element.7.y_hbm, bf16[4,16,1792]{2,1,0:T(8,128)(2,1)} %get-tuple-element.8.g_hbm, bf16[512,64]{1,0:T(8,128)(2,1)} %get-tuple-element.9.left_hbm), custom_call_target="tpu_custom_call" | custom-call | tf_op jit(solution)/shard_map/write_out/pallas_call | solution.py:539

commit v5 on v4

--- a/solution.py
+++ b/solution.py
@@ -25,13 +25,19 @@
     RIGHT: tuple((hops, j, 1) for hops, order in ((0, (0, 1, 3, 2)), (1, (0, 1, 3, 2)), (2, (0, 1, 3, 2)), (3, (0, 1))) for j in order),
     LEFT: tuple((hops, j, 1) for hops, order in ((0, (0, 3, 1, 2)), (1, (3, 0, 2, 1)), (2, (3, 2, 0, 1)), (3, (3, 2))) for j in order),
 }
-GRADS = ROWS
+GRADS = {
+    RIGHT: ROWS[RIGHT],
+    LEFT: tuple((hops, j, 1) for hops, order in ((0, (0, 3, 2, 1)), (1, (3, 2, 0, 1)), (2, (3, 2, 0, 1)), (3, (3, 2))) for j in order),
+}
 LAST = (1, 2, 3, 0)
 ENDS = {
     LEFT: tuple((hops, j, 1) for hops, order in ((4, (1, 3)), (3, (2, 0, 1, 3)), (2, (2, 1, 0, 3)), (1, LAST)) for j in order),
     RIGHT: tuple((hops, j, 1) for hops, order in ((4, (2, 0)), (3, (1, 3, 2, 0)), (2, (1, 3, 2, 0)), (1, LAST)) for j in order),
 }
-OUTS = ENDS
+OUTS = {
+    LEFT: tuple((hops, j, 1) for hops, order in ((4, (1, 3)), (3, (2, 0, 1, 3)), (2, (2, 0, 1, 3)), (1, (2, 0, 1, 3))) for j in order),
+    RIGHT: tuple((hops, j, 1) for hops, order in ((4, (2, 0)), (3, (1, 3, 2, 0)), (2, (1, 3, 2, 0)), (1, (1, 3, 2, 0))) for j in order),
+}
 STEPS = len(ENDS[LEFT])
 ORDERS = (ROWS, GRADS, OUTS, ENDS)
 MOST = max(len(order[way]) for order in ORDERS for way in WAYS)
@@ -228,33 +234,29 @@
         return (m == there).astype(F32).astype(BF16)
 
     def cols_of(i, q=0):
-        return pl.ds(pl.multiple_of(q * quarter + i * COLS, COLS), COLS)
+        start = q * quarter + i * COLS
+        return pl.ds(start if isinstance(start, int) else pl.multiple_of(start, COLS), COLS)
 
     def natural(buf, group):
-        def body(i, carry):
+        for i in range(quarter // COLS):
             block = buf[pl.ds(4 * group, 4), :, :, cols_of(i)].reshape(STACK * QUARTERS, COLS)
             got = dot(swap[...], block).astype(BF16)
             for q in range(QUARTERS):
                 nat[pl.ds(STACK * group, STACK), cols_of(i, q)] = got[q * STACK : (q + 1) * STACK]
-            return carry
-        lax.fori_loop(0, quarter // COLS, body, 0)
 
     def blocked(product, part, first, last):
-        def body(i, carry):
+        for i in range(first, last):
             pieces = [product(cols_of(i, q)).astype(BF16) for q in range(QUARTERS)]
             for group in range(count // STACK):
                 block = jnp.concatenate([p[STACK * group : STACK * (group + 1)] for p in pieces], axis=0)
                 got = tn(swap[...], block).astype(BF16)
                 part[pl.ds(4 * group, 4), :, :, cols_of(i)] = got.reshape(4, FLIGHT, UNIT, COLS)
-            return carry
-        lax.fori_loop(first, last, body, 0)
 
     def gate_up(first, last):
-        def body(i, carry):
-            ks = pl.ds(pl.multiple_of(i * TILE, TILE), TILE)
-            acc[...] += dot(nat[:, ks], gu[ks, :])
-            return carry
-        lax.fori_loop(first, last, body, 0)
+        ks = pl.ds(first * TILE, (last - first) * TILE)
+        for n in range(0, 4 * units, COLS):
+            cols = pl.ds(n, COLS)
+            acc[:, cols] += dot(nat[:, ks], gu[ks, cols])
 
     def activate():
         gate, upper = acc[:, : 2 * units], acc[:, 2 * units :]
@@ -268,11 +270,8 @@
         blocked(lambda cols: dot(hid[...], wd[:, cols]), part_y, first, last)
 
     def d_hidden(first, last):
-        def body(i, carry):
-            ks = pl.ds(pl.multiple_of(i * TILE, TILE), TILE)
-            dh[...] += nt(nat[:, ks], wd[:, ks])
-            return carry
-        lax.fori_loop(first, last, body, 0)
+        ks = pl.ds(first * TILE, (last - first) * TILE)
+        dh[...] += nt(nat[:, ks], wd[:, ks])
 
     def d_activate():
         dgu[:, : 2 * units] = (dh[...] * a_gate[...]).astype(BF16)
@@ -289,13 +288,11 @@
 
     def place(left, got, out):
         terms = left.shape[1] // STACK
-        def body(i, carry):
+        for i in range(quarter // COLS):
             block = got[:, :, cols_of(i)].reshape(STACK, COLS)
             total = dot(left, jnp.concatenate([block] * terms, axis=0)).astype(BF16)
             for q in range(QUARTERS):
                 out[:, cols_of(i, q)] = total[q * tokens : (q + 1) * tokens]
-            return carry
-        lax.fori_loop(0, quarter // COLS, body, 0)
 
     def three_terms(weights):
         high = weights.astype(BF16).astype(F32)
@@ -399,24 +396,41 @@
     d_inputs(0, 2)
     out_steps(6, 7)
     d_inputs(2, 4)
-    out_steps(8, 9)
+    out_steps(8)
     d_inputs(4, 6)
-    out_steps(10, 11)
+    out_steps(9)
     d_inputs(6, steps)
-    out_steps(12)
     end_steps(0, 1)
-    out_steps(13)
+    out_steps(10)
     end_steps(2, 3)
-
-    done_y = finish(2, part_y, recv_y, got_y, up, LAST)
-    end_steps(4, 5)
     small[0].wait_recv()
     weights_y = by_quarter(three_terms(wsel_in[...]))
     small[1].wait_recv()
     left_ref[...] = by_quarter(jnp.concatenate([sel_in[...], jnp.zeros_like(sel_in)], axis=0).T[:, :STACK])
+    out_steps(11)
+    end_steps(4, 5)
+    for copy in x_copies + g_copies + other + small:
+        copy.wait_send()
+    out_steps(12)
     end_steps(6, 7)
+    out_steps(13)
+    end_steps(8, 9, 10)
+    for i in range(STEPS):
+        for way in WAYS:
+            gather_copy(0, rows, ROWS, way, i).wait_send()
+            gather_copy(1, grads, GRADS, way, i).wait_send()
+
+    done_y = finish(2, part_y, recv_y, got_y, up, LAST)
+    end_steps(11, 12, 13)
+    for i in range(STEPS):
+        for way in WAYS:
+            sum_copy(2, part_y, recv_y, way, i).wait_send()
+    done_g = finish(3, part_g, recv_g, got_g, down, LAST)
+    for i in range(STEPS):
+        for way in WAYS:
+            sum_copy(3, part_g, recv_g, way, i).wait_send()
     for copy in done_y:
-        copy.wait_recv()
+        copy.wait()
     place(weights_y, got_y, out_ref)
     results = [
         pltpu.make_async_copy(out_ref, out_hbm, local_sems.at[7]),
@@ -424,19 +438,6 @@
     ]
     for copy in results:
         copy.start()
-    end_steps(8, 9)
-    for copy in x_copies + g_copies + other + small + done_y:
-        copy.wait_send()
-    end_steps(10, 11, 12, 13)
-    for i in range(STEPS):
-        for way in WAYS:
-            gather_copy(0, rows, ROWS, way, i).wait_send()
-            gather_copy(1, grads, GRADS, way, i).wait_send()
-            sum_copy(2, part_y, recv_y, way, i).wait_send()
-    done_g = finish(3, part_g, recv_g, got_g, down, LAST)
-    for i in range(STEPS):
-        for way in WAYS:
-            sum_copy(3, part_g, recv_g, way, i).wait_send()
     for copy in done_g + results:
         copy.wait()
 

time: 95.4 us -> 91.8 us (0.962)
  Pallas kernels: 94.6 us -> 91 us
    pallas_call x1, Pallas kernels: 91.3 us -> 87.6 us  [on_device(): pl.pallas_call(exchange, out_shape=(dense, jax.ShapeDtypeStruct((FLIGHT,...]
where the time goes in v5:
time: 91.8 us; the launch traced here: 91.6 us
  Pallas kernels  91 us (99%)
    pallas_call x1, Pallas kernels, on_device(): pl.pallas_call(exchange, out_shape=(dense, jax.ShapeDtypeStruct((FLIGHT,...  87.6 us
    pallas_call x1, Pallas kernels, on_device(): pl.pallas_call(write_out, out_shape=(dense,) * 2, in_specs=[hbm] * 3, out...  3.36 us

profile of v5, /device:TPU:24, one launch (start us, length us, event | category | flops | bytes accessed | tf_op | source)
XLA Modules:
  0.0 91.6 jit_solution(5008351390858673692)
XLA Ops:
  0.6 87.6 %exchange.1 = (bf16[128,7168]{1,0:T(8,128)(2,1)}, bf16[4,16,1792]{2,1,0:T(8,128)(2,1)}, bf16[512,64]{1,0:T(8,128)(2,1)}) custom-call(s32[8,128]{1,0:T(8,128)} %bitcast.20, s32[8,128]{1,0:T(8,128)} %bitcast.21, bf16[128,7168]{1,0:T(8,128)(2,1)} %bitcast.13, bf16[128,7168]{1,0:T(8,128)(2,1)} %bitcast.14, bf16[7168,128]{1,0:T(8,128)(2,1)} %bitcast.15, ...), custom_call_target="tpu_custom_call" | custom-call | flops 2818572288 | bytes 12845056 | tf_op jit(solution)/shard_map/exchange/pallas_call | solution.py:502
  88.3 3.4 %write_out.1 = (bf16[128,7168]{1,0:T(8,128)(2,1)}, bf16[128,7168]{1,0:T(8,128)(2,1)}) custom-call(bf16[128,7168]{1,0:T(8,128)(2,1)} %get-tuple-element.7.y_hbm, bf16[4,16,1792]{2,1,0:T(8,128)(2,1)} %get-tuple-element.8.g_hbm, bf16[512,64]{1,0:T(8,128)(2,1)} %get-tuple-element.9.left_hbm), custom_call_target="tpu_custom_call" | custom-call | tf_op jit(solution)/shard_map/write_out/pallas_call | solution.py:540

commit v6 on v5

--- a/solution.py
+++ b/solution.py
@@ -6,6 +6,7 @@
 from jax.sharding import PartitionSpec as P
 
 CAP = 4
+TOP = 8
 FLIGHT = 4
 QUARTERS = 4
 CORES = 2
@@ -60,9 +61,9 @@
 
 
 def exchange(
-    routes_hbm, codes_hbm, tok_hbm, cot_hbm, wg_ref, wu_ref, wd_ref,
-    out_hbm, got_g, left_hbm,
-    out_ref, left_ref, routes_ref, codes_ref, tok, cot, pick_x, pick_g, rows, grads, nat, gu, wd, swap, acc, a_gate, a_up, hid, dh, dgu,
+    routing_ref, tok_hbm, cot_hbm, wg_ref, wu_ref, wd_ref,
+    out_ref, got_g, left_ref,
+    tok, cot, pick_x, pick_g, rows, grads, nat, gu, wd, swap, acc, a_gate, a_up, hid, dh, dgu,
     part_y, part_g, recv_y, recv_g, got_y, sel, wsel, sel_in, wsel_in,
     local_sems, w_send, w_recv, x_send, x_recv, s_send, s_recv,
     ring_send, ring_recv, fin_send, fin_recv,
@@ -94,16 +95,13 @@
     down = [at(xx, z, core, behind) for xx in plane]
 
     own = [
-        pltpu.make_async_copy(routes_hbm, routes_ref, local_sems.at[5]),
-        pltpu.make_async_copy(codes_hbm, codes_ref, local_sems.at[6]),
         pltpu.make_async_copy(tok_hbm, tok, local_sems.at[0]),
         pltpu.make_async_copy(cot_hbm, cot, local_sems.at[1]),
         pltpu.make_async_copy(wg_ref, gu.at[:, pl.ds(0, units)], local_sems.at[2]),
         pltpu.make_async_copy(wu_ref, gu.at[:, pl.ds(2 * units, units)], local_sems.at[3]),
         pltpu.make_async_copy(wd_ref, wd.at[pl.ds(0, units)], local_sems.at[4]),
     ]
-    for copy in own[:3]:
-        copy.start()
+    own[0].start()
 
     barrier = pltpu.get_barrier_semaphore()
     peers = [sibling, next_on[RIGHT], next_on[LEFT]] + across[1:] + up + down
@@ -116,10 +114,8 @@
             device_id=device, device_id_type=MESH,
         )
 
-    own[0].wait()
-    own[1].wait()
-    routes = routes_ref[...]
-    codes = codes_ref[...].astype(F32)
+    routes = routing_ref[:TOP]
+    codes = routing_ref[TOP:].astype(F32)
     ratio = 2.5 * codes / jnp.sum(codes, axis=0, keepdims=True)
     named = [routes == f for f in range(FLIGHT)]
     matched = [jnp.sum(jnp.where(hit, 1.0, 0.0), axis=0, keepdims=True) for hit in named]
@@ -304,8 +300,8 @@
     tiles = width // TILE
     steps = quarter // COLS
 
-    own[2].wait()
-    own[3].start()
+    own[0].wait()
+    own[1].start()
     choose(tok, pick_x, None, 0, steps)
     pl.semaphore_wait(barrier, len(peers))
     x_copies = [x_copy(0, pick_x, rows, k) for k in (1, 3, 2)]
@@ -329,8 +325,8 @@
             sum_step(3, part_g, recv_g, i)
 
     row_steps(0)
-    own[3].wait()
-    for copy in own[4:]:
+    own[1].wait()
+    for copy in own[2:]:
         copy.start()
     choose(cot, pick_g, jnp.sum(wsel[...], axis=1, keepdims=True), 0, steps)
     g_copies = [x_copy(1, pick_g, grads, k) for k in (1, 3, 2)]
@@ -365,7 +361,7 @@
 
     gather_end(0, pick_x, rows, ROWS)
     natural(rows, 1)
-    for copy in own[4:]:
+    for copy in own[2:]:
         copy.wait()
     for copy in other:
         copy.wait_recv()
@@ -432,40 +428,16 @@
     for copy in done_y:
         copy.wait()
     place(weights_y, got_y, out_ref)
-    results = [
-        pltpu.make_async_copy(out_ref, out_hbm, local_sems.at[7]),
-        pltpu.make_async_copy(left_ref, left_hbm, local_sems.at[8]),
-    ]
-    for copy in results:
-        copy.start()
-    for copy in done_g + results:
+    for copy in done_g:
         copy.wait()
 
 
-def write_out(y_hbm, g_hbm, left_hbm, out_hbm, grad_hbm, y_ref, g_ref, left_ref, dense, in_sems, y_sems, sems):
-    tokens, width = y_hbm.shape
+def write_out(y_ref, g_ref, left_ref, out_hbm, grad_hbm, dense, sems):
+    tokens, width = y_ref.shape
     quarter = width // QUARTERS
-    needed = [
-        pltpu.make_async_copy(g_hbm, g_ref, in_sems.at[0]),
-        pltpu.make_async_copy(left_hbm, left_ref, in_sems.at[1]),
-    ]
-    for copy in needed:
-        copy.start()
-    part = tokens // QUARTERS
-    here = []
-    for n in range(QUARTERS):
-        rows = pl.ds(n * part, part)
-        here.append(pltpu.make_async_copy(y_hbm.at[rows], y_ref.at[rows], in_sems.at[2 + n]))
-        here[n].start()
-    for copy in needed:
-        copy.wait()
+    copies = [pltpu.make_async_copy(y_ref, out_hbm, sems.at[3 * QUARTERS])]
+    copies[0].start()
     left = left_ref[...]
-    copies = []
-    for n in range(QUARTERS):
-        rows = pl.ds(n * part, part)
-        here[n].wait()
-        copies.append(pltpu.make_async_copy(y_ref.at[rows], out_hbm.at[rows], y_sems.at[n]))
-        copies[n].start()
     cuts = (0, 3, 5, 7)
     for n in range(len(cuts) - 1):
         for i in range(cuts[n], cuts[n + 1]):
@@ -489,13 +461,13 @@
     quarter = width // QUARTERS
     units = w_gate.shape[2]
     count = RING * FLIGHT * CAP
+    vmem = pl.BlockSpec(memory_space=pltpu.VMEM)
     hbm = pl.BlockSpec(memory_space=pltpu.HBM)
     dma = pltpu.SemaphoreType.DMA
     blocks = pltpu.VMEM((FLIGHT, UNIT, quarter), BF16)
     gathered = pltpu.VMEM((RING, FLIGHT, UNIT, quarter), BF16)
     incoming = pltpu.VMEM((2, 4, FLIGHT, UNIT, quarter), BF16)
     block = pltpu.VMEM((tokens, width), BF16)
-    route = pltpu.VMEM(routes.shape[:0:-1], jnp.int32)
     half_wide = pltpu.VMEM((count, 2 * units), F32)
     select = pltpu.VMEM((STACK, tokens), F32)
     dense = jax.ShapeDtypeStruct((tokens, width), BF16)
@@ -506,10 +478,10 @@
             jax.ShapeDtypeStruct((FLIGHT, UNIT, quarter), BF16),
             jax.ShapeDtypeStruct((QUARTERS * tokens, STACK), BF16),
         ),
-        in_specs=[hbm] * 7,
-        out_specs=(hbm,) * 3,
+        in_specs=[vmem] + [hbm] * 5,
+        out_specs=(vmem,) * 3,
         scratch_shapes=[
-            block, pltpu.VMEM((QUARTERS * tokens, STACK), BF16), route, route, block, block, blocks, blocks, gathered, gathered,
+            block, block, blocks, blocks, gathered, gathered,
             pltpu.VMEM((count, width), BF16),
             pltpu.VMEM((width, 4 * units), BF16),
             pltpu.VMEM((2 * units, width), BF16),
@@ -522,7 +494,7 @@
             pltpu.VMEM((count, 4 * units), BF16),
             gathered, gathered, incoming, incoming, blocks,
             select, select, select, select,
-            dma((9,)),
+            dma((5,)),
             dma((3,)), dma((3,)),
             dma((2, FLIGHT)), dma((2, FLIGHT)),
             dma((2,)), dma((2,)),
@@ -530,23 +502,20 @@
             dma((2, FLIGHT)), dma((2, FLIGHT)),
         ],
         compiler_params=pltpu.CompilerParams(
-            collective_id=0, has_side_effects=True, vmem_limit_bytes=57 * 2**20
+            collective_id=0, has_side_effects=True, vmem_limit_bytes=51 * 2**20
         ),
         cost_estimate=pl.CostEstimate(
             flops=24 * count * width * units, bytes_accessed=14 * tokens * width, transcendentals=0
         ),
         name="exchange",
-    )(routes[0].T, gate_codes[0].T, section_input[0], cotangent[0], w_gate[0], w_up[0], w_down[0])
+    )(jnp.concatenate([routes[0].T, gate_codes[0].T]), section_input[0], cotangent[0], w_gate[0], w_up[0], w_down[0])
     passed, grad_passed = pl.pallas_call(
         write_out,
         out_shape=(dense,) * 2,
-        in_specs=[hbm] * 3,
+        in_specs=[vmem] * 3,
         out_specs=(hbm,) * 2,
-        scratch_shapes=[
-            block, blocks, pltpu.VMEM((QUARTERS * tokens, STACK), BF16), block,
-            dma((2 + QUARTERS,)), dma((QUARTERS,)), dma((3 * QUARTERS,)),
-        ],
-        compiler_params=pltpu.CompilerParams(vmem_limit_bytes=57 * 2**20),
+        scratch_shapes=[block, dma((1 + 3 * QUARTERS,))],
+        compiler_params=pltpu.CompilerParams(vmem_limit_bytes=51 * 2**20),
         name="write_out",
     )(out_dense, got_g, left)
     return passed[None], grad_passed[None]

time: 91.8 us -> 90.7 us (0.988)
  Pallas kernels: 91 us -> 89.2 us
    pallas_call x1, Pallas kernels: 3.36 us -> 1.93 us  [on_device(): pl.pallas_call(write_out, out_shape=(dense,) * 2, in_specs=[vmem] * 3, ou...]
where the time goes in v6:
time: 90.7 us; the launch traced here: 90.5 us
  Pallas kernels  89.2 us (98%)
    pallas_call x1, Pallas kernels, on_device(): pl.pallas_call(exchange, out_shape=(dense, jax.ShapeDtypeStruct((FLIGHT,...  87.3 us
    pallas_call x1, Pallas kernels, on_device(): pl.pallas_call(write_out, out_shape=(dense,) * 2, in_specs=[vmem] * 3, ou...  1.93 us

profile of v6, /device:TPU:24, one launch (start us, length us, event | category | flops | bytes accessed | tf_op | source)
XLA Modules:
  0.0 90.5 jit_solution(15852753221438394673)
XLA Ops:
  0.6 0.7 pad_add_fusion.routing_ref
  1.3 87.3 %exchange.1 = (bf16[128,7168]{1,0:T(8,128)(2,1)S(1)}, bf16[4,16,1792]{2,1,0:T(8,128)(2,1)S(1)}, bf16[512,64]{1,0:T(8,128)(2,1)S(1)}) custom-call(s32[16,128]{1,0:T(8,128)S(1)} %pad_add_fusion.routing_ref, bf16[128,7168]{1,0:T(8,128)(2,1)} %bitcast.15, bf16[128,7168]{1,0:T(8,128)(2,1)} %bitcast.16, bf16[7168,128]{1,0:T(8,128)(2,1)} %bitcast.17, ...), custom_call_target="tpu_custom_call" | custom-call | flops 2818572288 | bytes 12845056 | tf_op jit(solution)/shard_map/exchange/pallas_call | solution.py:474
  88.6 1.9 %write_out.1 = (bf16[128,7168]{1,0:T(8,128)(2,1)}, bf16[128,7168]{1,0:T(8,128)(2,1)}) custom-call(bf16[128,7168]{1,0:T(8,128)(2,1)S(1)} %get-tuple-element.7.y_ref, bf16[4,16,1792]{2,1,0:T(8,128)(2,1)S(1)} %get-tuple-element.8.g_ref, bf16[512,64]{1,0:T(8,128)(2,1)S(1)} %get-tuple-element.9.left_ref), custom_call_target="tpu_custom_call" | custom-call | tf_op jit(solution)/shard_map/write_out/pallas_call | solution.py:512

commit v7 on v6

--- a/solution.py
+++ b/solution.py
@@ -410,14 +410,14 @@
     out_steps(12)
     end_steps(6, 7)
     out_steps(13)
-    end_steps(8, 9, 10)
+    end_steps(8, 9, 10, 11)
     for i in range(STEPS):
         for way in WAYS:
             gather_copy(0, rows, ROWS, way, i).wait_send()
             gather_copy(1, grads, GRADS, way, i).wait_send()
 
     done_y = finish(2, part_y, recv_y, got_y, up, LAST)
-    end_steps(11, 12, 13)
+    end_steps(12, 13)
     for i in range(STEPS):
         for way in WAYS:
             sum_copy(2, part_y, recv_y, way, i).wait_send()

time: 90.7 us -> 90.7 us (level)
  no operation moved by 1% of the time
where the time goes in v7:
time: 90.7 us; the launch traced here: 90.5 us
  Pallas kernels  89.2 us (98%)
    pallas_call x1, Pallas kernels, on_device(): pl.pallas_call(exchange, out_shape=(dense, jax.ShapeDtypeStruct((FLIGHT,...  87.3 us
    pallas_call x1, Pallas kernels, on_device(): pl.pallas_call(write_out, out_shape=(dense,) * 2, in_specs=[vmem] * 3, ou...  1.93 us

profile of v7, /device:TPU:24, one launch (start us, length us, event | category | flops | bytes accessed | tf_op | source)
XLA Modules:
  0.0 90.5 jit_solution(18411994155425747812)
XLA Ops:
  0.6 0.7 pad_add_fusion.routing_ref
  1.3 87.3 %exchange.1 = (bf16[128,7168]{1,0:T(8,128)(2,1)S(1)}, bf16[4,16,1792]{2,1,0:T(8,128)(2,1)S(1)}, bf16[512,64]{1,0:T(8,128)(2,1)S(1)}) custom-call(s32[16,128]{1,0:T(8,128)S(1)} %pad_add_fusion.routing_ref, bf16[128,7168]{1,0:T(8,128)(2,1)} %bitcast.15, bf16[128,7168]{1,0:T(8,128)(2,1)} %bitcast.16, bf16[7168,128]{1,0:T(8,128)(2,1)} %bitcast.17, ...), custom_call_target="tpu_custom_call" | custom-call | flops 2818572288 | bytes 12845056 | tf_op jit(solution)/shard_map/exchange/pallas_call | solution.py:474
  88.6 1.9 %write_out.1 = (bf16[128,7168]{1,0:T(8,128)(2,1)}, bf16[128,7168]{1,0:T(8,128)(2,1)}) custom-call(bf16[128,7168]{1,0:T(8,128)(2,1)S(1)} %get-tuple-element.7.y_ref, bf16[4,16,1792]{2,1,0:T(8,128)(2,1)S(1)} %get-tuple-element.8.g_ref, bf16[512,64]{1,0:T(8,128)(2,1)S(1)} %get-tuple-element.9.left_ref), custom_call_target="tpu_custom_call" | custom-call | tf_op jit(solution)/shard_map/write_out/pallas_call | solution.py:512
